TPU v7x, 128 devices: a whole 4x4x4 slice. The times are simulated.
128 devices in a mesh: src: 16 (over x, y), grp: 8 (over z, core).
Axes of the slice: x: 4, y: 4, z: 4, core: 2. Of those that a mesh axis runs over, the one named last changes fastest.
Arguments:
- embeds: bfloat16 [131072, 768], P(('src', 'grp')), may hold values from -6 to 6
- cluster_id: int32 [131072], P(('src', 'grp')), may hold values from 0 to 47, as said below
- cluster_rank: int32 [131072], P(('src', 'grp')), may hold values from 0 to 8189, as said below
- cluster_size: int32 [48], replicated, may hold values from 1 to 8190, as said below
Outputs:
- best: float32 [131072], P(('src', 'grp'))
Inputs may be any that keep to these rules, and one draw needn't show every extreme that they name: `cluster_id`: every cluster id occurs; the clusters with ids g * 3 to g * 3 + 2 hold 8192 rows together. `cluster_rank`: within each cluster the ranks are 0 to its size minus one, each once. In the order by cluster and rank, no device's rows take more than 8 places of any aligned run of 512 places, and every aligned run of 1024 places has 16 places from some one device. cluster_size is the number of rows with each cluster id.
All inputs are finite; a program needn't handle non-finite values.
Results may differ from a plain program's by a relative error of at most 0.0013.
Values may be sent and summed in bfloat16 or wider, within the bound.
A program may use at most 128 MiB of HBM per device.

v0:
```python
import jax
import jax.numpy as jnp
from jax import lax
from jax.sharding import PartitionSpec as P

epsilon = 1e-06


def unit_vectors(embeds):
    widened = embeds.astype(jnp.float32)
    return (
        widened * lax.rsqrt(jnp.sum(widened * widened, axis=1, keepdims=True) + epsilon)
    ).astype(jnp.bfloat16)


def cluster_of(positions, starts):
    return jnp.sum((positions[:, None] >= starts[None, :]).astype(jnp.int32), axis=1) - 1


def held_positions(held_index, group_base):
    return group_base + held_index


def score_block(current, queries, query_pos, query_cl, key_rows, key_pos, key_cl):
    scores = lax.dot_general(
        queries, key_rows, (((1,), (1,)), ((), ())), preferred_element_type=jnp.float32
    )
    allowed = (key_cl[None, :] == query_cl[:, None]) & (key_pos[None, :] < query_pos[:, None])
    return jnp.maximum(current, jnp.max(jnp.where(allowed, scores, -1.0), axis=1))


def absorb(best_score, queries, query_pos, query_cl, key_rows, key_pos, key_cl):
    half_rows = best_score.shape[1]
    key_count = key_rows.shape[0]
    results = []
    for portion in range(2):
        offset_row = portion * half_rows
        part_rows = queries[offset_row : offset_row + half_rows]
        part_pos = query_pos[offset_row : offset_row + half_rows]
        part_cl = query_cl[offset_row : offset_row + half_rows]
        current = best_score[portion]
        for opening in range(0, key_count, half_rows):
            finish = min(opening + half_rows, key_count)
            block_rows = key_rows[opening:finish]
            block_pos = key_pos[opening:finish]
            block_cl = key_cl[opening:finish]
            current = score_block(
                current, part_rows, part_pos, part_cl, block_rows, block_pos, block_cl
            )
        results.append(current)
    return jnp.stack(results)


def fold_group(held_units, combine, initial):
    return combine(initial, lax.all_gather(held_units, "grp", axis=0, tiled=True), jnp.int32(0))


def on_device(embeds, cluster_id, cluster_rank, cluster_size):
    row_count = embeds.shape[0]
    half_rows = row_count // 2
    feature_count = embeds.shape[1]
    group_count = lax.axis_size("grp")
    source_count = lax.axis_size("src")
    device_count = source_count * group_count
    capacity = 2 * row_count // device_count
    group_rows = group_count * row_count
    group_base = lax.axis_index("src") * group_rows
    own_index = lax.axis_index("grp")
    unit_rows = unit_vectors(embeds)
    starts = jnp.cumsum(cluster_size) - cluster_size
    labels = jnp.arange(cluster_size.shape[0], dtype=jnp.int32)
    position = (
        jnp.sum(jnp.where(cluster_id[:, None] == labels[None, :], starts[None, :], 0), axis=1)
        + cluster_rank
    )
    within = position % group_rows
    owner = within // row_count
    target_row = within % row_count
    target_device = position // group_rows * group_count + owner
    chosen = (target_device[:, None] == jnp.arange(device_count, dtype=jnp.int32)[None, :]).astype(
        jnp.int32
    )
    slot_index = jnp.sum((jnp.cumsum(chosen, axis=0) - 1) * chosen, axis=1)
    send_units = (
        jnp.zeros((device_count, capacity, feature_count), jnp.bfloat16)
        .at[target_device, slot_index]
        .set(unit_rows)
    )
    send_rows = (
        jnp.full((device_count, capacity), row_count, jnp.int32)
        .at[target_device, slot_index]
        .set(target_row)
    )
    got_units, got_rows = (
        lax.all_to_all(send_units, ("src", "grp"), split_axis=0, concat_axis=0, tiled=True),
        lax.all_to_all(send_rows, ("src", "grp"), split_axis=0, concat_axis=0, tiled=True),
    )
    held_units = (
        jnp.zeros((row_count, feature_count), jnp.bfloat16)
        .at[got_rows.reshape(-1)]
        .set(got_units.reshape(-1, feature_count), mode="drop")
    )
    query_pos = held_positions(
        own_index * row_count + jnp.arange(row_count, dtype=jnp.int32), group_base
    )
    query_cl = cluster_of(query_pos, starts)
    best_score = jnp.full((2, half_rows), -1.0, jnp.float32)

    def take_piece(carried, key_piece, first_row):
        held_index = jnp.arange(key_piece.shape[0], dtype=jnp.int32)
        piece_pos = held_positions(held_index, group_base)
        return absorb(
            carried,
            held_units,
            query_pos,
            query_cl,
            key_piece,
            piece_pos,
            cluster_of(piece_pos, starts),
        )

    best_score = fold_group(held_units, take_piece, best_score)
    flat_best = best_score.reshape(row_count)
    answers = jnp.take(flat_best, jnp.minimum(got_rows, row_count - 1), axis=0)
    returned = lax.all_to_all(answers, ("src", "grp"), split_axis=0, concat_axis=0, tiled=True)
    return returned[target_device, slot_index]


def solution(mesh):
    placed = (P(("src", "grp"), None), P(("src", "grp")), P(("src", "grp")), P())
    return jax.shard_map(
        on_device, mesh=mesh, in_specs=placed, out_specs=P(("src", "grp")), check_vma=False
    )
```

profile of v0, /device:TPU:1, one launch (start us, length us, event | category | flops | bytes accessed | tf_op | source)
XLA Modules:
  0.0 231.7 jit_solution(17161287288589206871)
XLA Ops:
  6.5 0.7 copy.25
  7.5 0.7 sub.29
  8.1 0.8 convert_reduce_fusion.1
  8.9 0.7 compare_select_fusion.4
  10.8 4.3 %scatter_custom_fusion.1 = s32[2048]{0:T(1024)S(1)} fusion(s32[1024]{0:T(1024)S(1)} %get-tuple-element.51, s32[1024]{0:T(1024)S(1)} %get-tuple-element.43, s32[]{:T(128)} %constant.86.clone.1), kind=kCustom, calls=%fused_computation.150 | custom fusion | bytes 8196
  15.2 0.7 copy.28
  15.9 11.5 %all-to-all-start = ((s32[128,1,16]{2,1,0:T(1,128)}), s32[128,1,16]{2,1,0:T(1,128)S(1)}, u32[]{:S(2)}, u32[]{:S(2)}) async-start(s32[128,1,16]{2,1,0:T(1,128)} %copy.28), calls=%async_computation | async-start | bytes 131072 | tf_op jit(solution)/shard_map/all_to_all | solution.py:96
  27.8 7.7 %scatter_custom_fusion.2 = bf16[2048,768]{1,0:T(8,128)(2,1)} fusion(s32[1024]{0:T(1024)S(1)} %get-tuple-element.50, bf16[1024,768]{1,0:T(8,128)(2,1)S(1)} %copy-done.1, bf16[]{:T(256)} %constant.101.clone.1, f32[1024]{0:T(1024)S(1)} %add_rsqrt_fusion), kind=kCustom, calls=%fused_computation.9 | custom fusion | flops 2359296 | bytes 4722690
  35.5 1.2 all-to-all-done
  36.7 8.5 %all-to-all-start.1 = ((bf16[128,16,768]{2,1,0:T(8,128)(2,1)}), bf16[128,16,768]{2,1,0:T(8,128)(2,1)S(1)}, u32[]{:S(2)}, u32[]{:S(2)}) async-start(bf16[128,16,768]{2,1,0:T(8,128)(2,1)} %bitcast.12), calls=%async_computation.1 | async-start | bytes 6291456 | tf_op jit(solution)/shard_map/all_to_all | solution.py:95
  45.8 0.8 reduce.11
  46.8 40.4 %all-to-all-done.1 = bf16[128,16,768]{2,1,0:T(8,128)(2,1)S(1)} async-done(((bf16[128,16,768]{2,1,0:T(8,128)(2,1)}), bf16[128,16,768]{2,1,0:T(8,128)(2,1)S(1)}, u32[]{:S(2)}, u32[]{:S(2)}) %all-to-all-start.1) | async-done | bytes 3145760 | tf_op jit(solution)/shard_map/all_to_all | solution.py:95
  87.1 11.0 %scatter_custom_fusion = bf16[1024,768]{1,0:T(8,128)(2,1)} fusion(s32[2048]{0:T(1024)S(1)} %bitcast.49, bf16[2048,768]{1,0:T(8,128)(2,1)S(1)} %bitcast.39, bf16[]{:T(256)} %constant.101.clone.1), kind=kCustom, calls=%fused_computation.77 | custom fusion | bytes 1572866 | tf_op jit(solution)/shard_map/scatter | solution.py:101
  98.6 63.5 %all-gather.2.cloned.1.call-done = bf16[8192,768]{1,0:T(8,128)(2,1)} async-done(((bf16[1024,768]{1,0:T(8,128)(2,1)}), bf16[8192,768]{1,0:T(8,128)(2,1)}) %all-gather.2.cloned.1.call-update) | async-done | bytes 12582928 | tf_op jit(solution)/shard_map/all_gather | solution.py:55
  162.1 1.9 fusion.22
  164.0 2.3 fusion.23
  166.3 1.8 fusion.24
  168.8 0.7 fusion.26
  170.7 0.7 fusion.29
  172.7 0.7 fusion.32
  181.9 0.9 fusion.14
  187.4 8.6 %gather_fusion = f32[2048]{0:T(1024)S(1)} fusion(f32[1024]{0:T(1024)S(1)} %bitcast.36, s32[2048]{0:T(1024)S(1)} %broadcast_clamp_fusion), kind=kCustom, calls=%fused_computation | custom fusion | bytes 24576 | tf_op jit(solution)/shard_map/jit(_take)/gather | solution.py:124
  196.1 17.3 %all_to_all.23 = f32[128,1,16]{2,1,0:T(1,128)S(1)} all-to-all(f32[128,1,16]{2,1,0:T(1,128)S(1)} %bitcast.42), channel_id=1, replica_groups=mesh['src'=16,'grp'=8] {'src','grp'}, dimensions={0} | all-to-all | bytes 16384 | tf_op jit(solution)/shard_map/all_to_all | solution.py:125
  213.4 11.5 %gather_fusion.1 = f32[1024]{0:T(1024)} fusion(f32[128,16]{0,1:T(8,128)S(1)} %bitcast.37, s32[1024]{0:T(1024)S(1)} %bitcast.38), kind=kCustom, calls=%fused_computation.1 | custom fusion | bytes 16384 | tf_op jit(solution)/shard_map/gather | solution.py:126
  (75 shorter events, 19.2 us)
Async XLA Ops:
  9.8 0.8 copy-start.4
  9.8 0.9 copy-start.2
  9.8 0.9 copy-start.3
  10.0 17.4 %copy-start.1 = (bf16[1024,768]{1,0:T(8,128)(2,1)S(1)}, bf16[1024,768]{1,0:T(8,128)(2,1)}, u32[]{:S(2)}) copy-start(bf16[1024,768]{1,0:T(8,128)(2,1)} %param.4) | copy-start | bytes 4718596
  15.9 20.9 %all-to-all-start = ((s32[128,1,16]{2,1,0:T(1,128)}), s32[128,1,16]{2,1,0:T(1,128)S(1)}, u32[]{:S(2)}, u32[]{:S(2)}) async-start(s32[128,1,16]{2,1,0:T(1,128)} %copy.28), calls=%async_computation | async-start | bytes 131072 | tf_op jit(solution)/shard_map/all_to_all | solution.py:96
  36.7 50.4 %all-to-all-start.1 = ((bf16[128,16,768]{2,1,0:T(8,128)(2,1)}), bf16[128,16,768]{2,1,0:T(8,128)(2,1)S(1)}, u32[]{:S(2)}, u32[]{:S(2)}) async-start(bf16[128,16,768]{2,1,0:T(8,128)(2,1)} %bitcast.12), calls=%async_computation.1 | async-start | bytes 6291456 | tf_op jit(solution)/shard_map/all_to_all | solution.py:95
  45.3 116.8 %all-gather.2.cloned.1.call-start = ((), (), s32[]{:S(2)}) async-start(), calls=%async_computation.3 | async-start | bytes 14155776 | tf_op jit(solution)/shard_map/all_gather | solution.py:55
  98.1 64.0 %copy-start = (bf16[1024,768]{1,0:T(8,128)(2,1)S(1)}, bf16[1024,768]{1,0:T(8,128)(2,1)}, u32[]{:S(2)}) copy-start(bf16[1024,768]{1,0:T(8,128)(2,1)} %scatter_custom_fusion) | copy-start | bytes 4718596
  162.1 6.0 %copy-start.5 = (bf16[8192,768]{1,0:T(8,128)(2,1)S(1)}, bf16[8192,768]{1,0:T(8,128)(2,1)}, u32[]{:S(2)}) copy-start(bf16[8192,768]{1,0:T(8,128)(2,1)} %all-gather.2.cloned.1.call-done) | copy-start | bytes 37748740
Sparse Core Ops, SparseCore 0:
  98.3 63.8 all-gather.1
where the time goes:
time: 232 us
  waiting for transfers between devices  105 us (45%)
  local copies, waits for them, and re-layouts  37.9 us (16%)
  matrix products  25.1 us (11%)
  starting transfers between devices  20.1 us (9%)
  blocking collectives  17.3 us (7%)
  between operations  13.8 us (6%)
  other arithmetic  12.5 us (5%)
    all_gather x1, waiting for transfers between devices, fold_group(): lax.all_gather(held_units, 'grp', axis=0, tiled=True)  63.5 us
    all_to_all x1, waiting for transfers between devices, on_device(): lax.all_to_all(send_units, ('src', 'grp'), split_axis=0, concat_axis=0, t...  40.4 us
    dot_general x32, matrix products, score_block(): lax.dot_general(queries, key_rows, (((1,), (1,)), ((), ())), preferred_el...  25.1 us
    all_to_all x1, blocking collectives, on_device(): lax.all_to_all(answers, ('src', 'grp'), split_axis=0, concat_axis=0, tile...  17.3 us
    all_to_all x1, starting transfers between devices, on_device(): lax.all_to_all(send_rows, ('src', 'grp'), split_axis=0, concat_axis=0, ti...  11.5 us
    gather x1, local copies, waits for them, and re-layouts, on_device(): return returned[target_device, slot_index]  11.5 us
    scatter x1, local copies, waits for them, and re-layouts, on_device(): held_units = jnp.zeros((row_count, feature_count), jnp.bfloat16).at[got_r...  11 us
    gather x2, local copies, waits for them, and re-layouts, on_device(): answers = jnp.take(flat_best, jnp.minimum(got_rows, row_count - 1), axis=0)  8.66 us
  transfers between devices with their start and end apart: 3, of which 3 were waited for; matrix products, arithmetic and copies ran while one was open for 4% of the time, Pallas kernels for 0%

commit v1 on v0

v1 whole, which is shorter than its diff:
```python
import functools

import jax
import jax.numpy as jnp
from jax import lax
from jax.experimental import pallas as pl
from jax.experimental.pallas import tpu as pltpu
from jax.sharding import PartitionSpec as P

MESH = pl.DeviceIdType.MESH
F32 = jnp.float32
BF16 = jnp.bfloat16

epsilon = 1e-06

DEVICES = 128
SLOTS = 16
CLASSES = 4
PER = DEVICES // CLASSES
CLASS_ROWS = PER * SLOTS
HALF = 512
MIX, UNMIX = 53, 29

NN = (((1,), (0,)), ((), ()))
NT = (((1,), (1,)), ((), ()))


def dot(a, b, dims=NN):
    return lax.dot_general(a, b, dims, preferred_element_type=F32)


def one_hot(mask):
    return jnp.where(mask, 1.0, 0.0).astype(BF16)


def iota(shape, dim):
    return lax.broadcasted_iota(jnp.int32, shape, dim)


def three_parts(x):
    first = x.astype(BF16)
    rest = x - first.astype(F32)
    second = rest.astype(BF16)
    third = (rest - second.astype(F32)).astype(BF16)
    return first, second, third


def kernel(
    embeds,
    ids,
    ranks,
    sizes,
    out,
    unit,
    send,
    recv,
    send_meta,
    recv_meta,
    place_of,
    gathered,
    blocks,
    tops,
    lows,
    others,
    answers,
    returned,
    send_sem,
    recv_sem,
    meta_send_sem,
    meta_recv_sem,
    block_send_sem,
    block_recv_sem,
    top_send_sem,
    top_recv_sem,
    answer_send_sem,
    answer_recv_sem,
):
    rows, width = embeds.shape
    src = lax.axis_index("src")
    grp = lax.axis_index("grp")
    x, y = src // 4, src % 4
    z, core = grp // 2, grp % 2

    def at_offset(step, sign):
        k = (step * MIX) % DEVICES
        dx, dy, dz, dc = k // 32, (k // 8) % 4, (k // 2) % 4, k % 2
        to_x = (x + sign * dx + 4) % 4
        to_y = (y + sign * dy + 4) % 4
        to_z = (z + sign * dz + 4) % 4
        return (to_x * 4 + to_y, to_z * 2 + (core + dc) % 2)

    barrier = pltpu.get_barrier_semaphore()

    def greet(step, carry):
        pl.semaphore_signal(barrier, inc=1, device_id=at_offset(step, 1), device_id_type=MESH)
        return carry

    lax.fori_loop(1, DEVICES, greet, 0)

    clusters = sizes.shape[1]
    size_row = sizes[...].astype(F32)
    earlier = iota((clusters, clusters), 1) < iota((clusters, clusters), 0)
    starts = jnp.sum(jnp.where(earlier, size_row, 0.0), axis=1, keepdims=True)
    mine = iota((clusters, rows), 0) == ids[...]
    start_row = jnp.sum(jnp.where(mine, starts, 0.0), axis=0, keepdims=True)
    position = start_row.astype(jnp.int32) + ranks[...]
    to_src = position >> 13
    to_grp = (position >> 10) & 7
    dx = ((to_src >> 2) - x) & 3
    dy = ((to_src & 3) - y) & 3
    dz = ((to_grp >> 1) - z) & 3
    dc = (to_grp - core) & 1
    step_row = ((dx * 32 + dy * 8 + dz * 2 + dc) * UNMIX) & (DEVICES - 1)
    to_step = one_hot(iota((DEVICES, rows), 0) == step_row)

    part = 256
    before = one_hot(iota((part, part), 0) < iota((part, part), 1))
    carry = jnp.zeros((DEVICES, 1), F32)
    slot_parts = []
    for n in range(rows // part):
        piece = to_step[:, n * part : (n + 1) * part]
        piece32 = piece.astype(F32)
        count = dot(piece, before) + carry
        slot_parts.append(jnp.sum(piece32 * count, axis=0, keepdims=True))
        carry = carry + jnp.sum(piece32, axis=1, keepdims=True)
    slot_row = jnp.concatenate(slot_parts, axis=1).astype(jnp.int32)
    index_row = step_row * SLOTS + slot_row
    lane_hot = one_hot(iota((DEVICES, rows), 0) == (index_row & (DEVICES - 1)))

    place_row = (position & (rows - 1)) + 1
    upper = to_step * (place_row >> 3).astype(F32).astype(BF16)
    lower = to_step * (place_row & 7).astype(F32).astype(BF16)
    meta = 8.0 * dot(upper, lane_hot, NT) + dot(lower, lane_hot, NT)
    send_meta[...] = meta.reshape(DEVICES, 1, DEVICES)
    recv_meta[0] = send_meta[0]

    pl.semaphore_wait(barrier, DEVICES - 1)

    def send_meta_step(step, carry):
        pltpu.make_async_remote_copy(
            src_ref=send_meta.at[step],
            dst_ref=recv_meta.at[step],
            send_sem=meta_send_sem,
            recv_sem=meta_recv_sem,
            device_id=at_offset(step, 1),
            device_id_type=MESH,
        ).start()
        return carry

    lax.fori_loop(1, DEVICES, send_meta_step, 0)

    def normalise(n, carry):
        here = pl.ds(pl.multiple_of(n * part, part), part)
        wide = embeds[here, :].astype(F32)
        total = jnp.sum(wide * wide, axis=1, keepdims=True)
        unit[here, :] = (wide * lax.rsqrt(total + epsilon)).astype(BF16)
        return carry

    lax.fori_loop(0, rows // part, normalise, 0)

    for n in range(CLASSES):
        pick = one_hot(iota((CLASS_ROWS, rows), 0) + n * CLASS_ROWS == index_row)
        packed = dot(pick, unit[...]).astype(BF16)
        send[pl.ds(n * PER, PER)] = packed.reshape(PER, SLOTS, width)
        if n == 0:
            recv[0] = send[0]

        def send_step(step, carry):
            pltpu.make_async_remote_copy(
                src_ref=send.at[step],
                dst_ref=recv.at[step],
                send_sem=send_sem.at[n],
                recv_sem=recv_sem.at[n],
                device_id=at_offset(step, 1),
                device_id_type=MESH,
            ).start()
            return carry

        lax.fori_loop(max(1, n * PER), (n + 1) * PER, send_step, 0)

    def wait_all(ref, sem, count):
        pltpu.make_async_copy(ref.at[pl.ds(1, count)], ref.at[pl.ds(1, count)], sem).wait()

    wait_all(recv_meta, meta_recv_sem, DEVICES - 1)

    got_places = jnp.sum(recv_meta[...].reshape(DEVICES // 8, 8, DEVICES), axis=1)
    got_places = got_places.astype(jnp.int32)
    for n in range(CLASSES):
        for m in range(CLASS_ROWS // DEVICES):
            line = n * (CLASS_ROWS // DEVICES) + m
            hit = iota((rows, DEVICES), 0) + 1 == got_places[line : line + 1, :]
            place_of[n, :, m * DEVICES : (m + 1) * DEVICES] = one_hot(hit)

    source_hot = jnp.zeros((DEVICES, rows), F32)
    lane_of = jnp.zeros((rows, DEVICES), F32)
    for n in range(CLASSES):
        group = one_hot(
            (iota((DEVICES, CLASS_ROWS), 1) + n * CLASS_ROWS) // SLOTS
            == iota((DEVICES, CLASS_ROWS), 0)
        )
        source_hot += dot(group, place_of[n], NT)
        for m in range(CLASS_ROWS // DEVICES):
            lane_of += place_of[n, :, m * DEVICES : (m + 1) * DEVICES].astype(F32)
    source_hot = source_hot.astype(BF16)
    lane_of = lane_of.astype(BF16)

    base = src * (8 * rows)
    after, prior = (z + 1) % 4, (z + 3) % 4
    crossed = z // 2
    prior_core = (core + crossed) % 2
    held = (z * 2, z * 2 + 1, after * 2 + core, prior * 2 + prior_core)
    for slot in range(4):
        for half in range(2):
            spot = held[slot] * rows + half * HALF
            places = (spot + base + iota((1, HALF), 1)).astype(F32)
            low = jnp.max(jnp.where(starts <= places, starts, 0.0), axis=0, keepdims=True)
            lows[slot * 2 + half] = low.astype(jnp.int32) - base
            tops[slot * 2 + half] = jnp.full((1, HALF), -1.0, F32)

    to_peer = (src, z * 2 + (core + 1) % 2)
    to_prior = (src, prior * 2 + core)
    to_after = (src, after * 2 + (core + after // 2) % 2)

    def block_copies(half):
        mine = blocks.at[core, half]
        for n, (slot, device) in enumerate(((core, to_peer), (2, to_prior), (3, to_after))):
            yield pltpu.make_async_remote_copy(
                src_ref=mine,
                dst_ref=blocks.at[slot, half],
                send_sem=block_send_sem.at[n, half],
                recv_sem=block_recv_sem.at[n, half],
                device_id=device,
                device_id_type=MESH,
            )

    for n in range(CLASSES):
        first = 1 if n == 0 else 0
        group = recv.at[pl.ds(n * PER + first, PER - first)]
        pltpu.make_async_copy(group, group, recv_sem.at[n]).wait()
        arrived = recv[pl.ds(n * PER, PER)].reshape(CLASS_ROWS, width)
        for half in range(2):
            here = pl.ds(half * HALF, HALF)
            found = dot(place_of[n, here, :], arrived)
            if n == 0:
                gathered[here, :] = found
            elif n < CLASSES - 1:
                gathered[here, :] += found
            else:
                blocks[core, half] = (gathered[here, :] + found).astype(BF16)
                for copy in block_copies(half):
                    copy.start()

    def spot_of(slot, half):
        number = z * 2 + slot
        number = jnp.where(slot == 2, held[2], number)
        number = jnp.where(slot == 3, held[3], number)
        return number * rows + half * HALF

    def score(key_slot, key_half, query_slot, query_half, same):
        products = dot(blocks[key_slot, key_half], blocks[query_slot, query_half], NT)
        line = query_slot * 2 + query_half
        key_no = iota((HALF, HALF), 0)
        allowed = key_no >= lows[line] - spot_of(key_slot, key_half)
        if same:
            allowed = allowed & (key_no < iota((HALF, HALF), 1))
        found = jnp.max(jnp.where(allowed, products, -1.0), axis=0, keepdims=True)
        tops[line] = jnp.maximum(tops[line], found)

    def score_pair(slot_a, half_a, slot_b, half_b):
        a_first = spot_of(slot_a, half_a) < spot_of(slot_b, half_b)
        key_slot = jnp.where(a_first, slot_a, slot_b)
        key_half = jnp.where(a_first, half_a, half_b)
        query_slot = jnp.where(a_first, slot_b, slot_a)
        query_half = jnp.where(a_first, half_b, half_a)
        score(key_slot, key_half, query_slot, query_half, False)

    def own_step(half, carry):
        score(core, half, core, half, True)
        return carry

    lax.fori_loop(0, 2, own_step, 0)

    def wait_block(n, half):
        list(block_copies(half))[n].wait_recv()

    for half in range(2):
        wait_block(0, half)

    def own_pairs(n, carry):
        plain = n == 2
        key_slot = jnp.where(plain, core, 0)
        key_half = jnp.where(plain, 0, n)
        query_slot = jnp.where(plain, core, 1)
        query_half = jnp.where(plain, 1, core)
        score(key_slot, key_half, query_slot, query_half, False)
        return carry

    lax.fori_loop(0, 3, own_pairs, 0)

    for half in range(2):
        wait_block(1, half)

        def with_after(n, carry):
            score_pair(n // 2, n % 2, 2, half)
            return carry

        lax.fori_loop(0, 4, with_after, 0)
        wait_block(2, half)

        def across(n, carry):
            number = n + half
            score_pair(3, number // 2, 2, number % 2)
            return carry

        lax.fori_loop(0, 1 + 2 * half, across, 0)

    back_prior = (src, prior * 2 + prior_core)
    back_after = (src, after * 2 + core)
    top_copies = []
    for n, (slot, device) in enumerate(
        (((core + 1) % 2, to_peer), (2, back_after), (3, back_prior))
    ):
        copy = pltpu.make_async_remote_copy(
            src_ref=tops.at[pl.ds(slot * 2, 2)],
            dst_ref=others.at[n],
            send_sem=top_send_sem.at[n],
            recv_sem=top_recv_sem.at[n],
            device_id=device,
            device_id_type=MESH,
        )
        copy.start()
        top_copies.append(copy)
    for copy in top_copies:
        copy.wait()
    halves = []
    for half in range(2):
        found = tops[core * 2 + half]
        for n in range(3):
            found = jnp.maximum(found, others[n, half])
        halves.append(found)
    best = jnp.concatenate(halves, axis=1)

    answer = jnp.zeros((DEVICES, DEVICES), F32)
    for piece in three_parts(best):
        answer += dot(source_hot * piece, lane_of)
    answers[...] = answer.reshape(DEVICES, 1, DEVICES)
    returned[0] = answers[0]

    def answer_step(step, carry):
        pltpu.make_async_remote_copy(
            src_ref=answers.at[step],
            dst_ref=returned.at[step],
            send_sem=answer_send_sem,
            recv_sem=answer_recv_sem,
            device_id=at_offset(step, -1),
            device_id_type=MESH,
        ).start()
        return carry

    lax.fori_loop(1, DEVICES, answer_step, 0)
    wait_all(returned, answer_recv_sem, DEVICES - 1)
    table = returned[...].reshape(DEVICES, DEVICES).T
    chosen = jnp.zeros((DEVICES, rows), F32)
    for piece in three_parts(table):
        chosen += dot(piece, to_step)
    out[...] = jnp.sum(chosen * lane_hot.astype(F32), axis=0, keepdims=True)

    wait_all(send_meta, meta_send_sem, DEVICES - 1)
    wait_all(answers, answer_send_sem, DEVICES - 1)
    for n in range(CLASSES):
        first = 1 if n == 0 else 0
        group = send.at[pl.ds(n * PER + first, PER - first)]
        pltpu.make_async_copy(group, group, send_sem.at[n]).wait()
    for half in range(2):
        for copy in block_copies(half):
            copy.wait_send()


def on_device(embeds, cluster_id, cluster_rank, cluster_size):
    rows, width = embeds.shape
    vmem = pl.BlockSpec(memory_space=pltpu.VMEM)
    best = pl.pallas_call(
        kernel,
        out_shape=jax.ShapeDtypeStruct((1, rows), F32),
        in_specs=[vmem] * 4,
        out_specs=vmem,
        scratch_shapes=[
            pltpu.VMEM((rows, width), BF16),
            pltpu.VMEM((DEVICES, SLOTS, width), BF16),
            pltpu.VMEM((DEVICES, SLOTS, width), BF16),
            pltpu.VMEM((DEVICES, 1, DEVICES), F32),
            pltpu.VMEM((DEVICES, 1, DEVICES), F32),
            pltpu.VMEM((CLASSES, rows, CLASS_ROWS), BF16),
            pltpu.VMEM((rows, width), F32),
            pltpu.VMEM((4, 2, HALF, width), BF16),
            pltpu.VMEM((8, 1, HALF), F32),
            pltpu.VMEM((8, 1, HALF), jnp.int32),
            pltpu.VMEM((3, 2, 1, HALF), F32),
            pltpu.VMEM((DEVICES, 1, DEVICES), F32),
            pltpu.VMEM((DEVICES, 1, DEVICES), F32),
            pltpu.SemaphoreType.DMA((CLASSES,)),
            pltpu.SemaphoreType.DMA((CLASSES,)),
            pltpu.SemaphoreType.DMA,
            pltpu.SemaphoreType.DMA,
            pltpu.SemaphoreType.DMA((3, 2)),
            pltpu.SemaphoreType.DMA((3, 2)),
            pltpu.SemaphoreType.DMA((3,)),
            pltpu.SemaphoreType.DMA((3,)),
            pltpu.SemaphoreType.DMA,
            pltpu.SemaphoreType.DMA,
        ],
        compiler_params=pltpu.CompilerParams(
            collective_id=0, has_side_effects=True, vmem_limit_bytes=50 * 1024 * 1024
        ),
        name="dedup",
    )(
        embeds,
        cluster_id.reshape(1, rows),
        cluster_rank.reshape(1, rows),
        cluster_size.reshape(1, -1),
    )
    return best.reshape(rows)


def solution(mesh):
    placed = (P(("src", "grp"), None), P(("src", "grp")), P(("src", "grp")), P())
    return jax.shard_map(
        on_device, mesh=mesh, in_specs=placed, out_specs=P(("src", "grp")), check_vma=False
    )
```

time: 232 us -> 118 us (0.51)
  Pallas kernels: 0 us -> 114 us
  waiting for transfers between devices: 105 us -> 0 us
  local copies, waits for them, and re-layouts: 37.9 us -> 4.03 us
  matrix products: 25.1 us -> 0 us
  starting transfers between devices: 20.1 us -> 0 us
  blocking collectives: 17.3 us -> 0 us
  between operations: 13.8 us -> 0.01 us
  other arithmetic: 12.5 us -> 0 us
    pallas_call x0 -> x1, Pallas kernels: none -> 114 us  [on_device(): pl.pallas_call(kernel, out_shape=jax.ShapeDtypeStruct((1, rows), F32), in...]
    all_gather x1 -> x0, waiting for transfers between devices: 63.5 us -> none  [fold_group(): lax.all_gather(held_units, 'grp', axis=0, tiled=True)]
    all_to_all x2 -> x0, waiting for transfers between devices: 41.6 us -> none  [the longest x1 40.4 us: on_device(): lax.all_to_all(send_units, ('src', 'grp'), split_axis=0, concat_axis=0, t...]
    dot_general x32 -> x0, matrix products: 25.1 us -> none  [score_block(): lax.dot_general(queries, key_rows, (((1,), (1,)), ((), ())), preferred_el...]
    gather x3 -> x0, local copies, waits for them, and re-layouts: 20.1 us -> none  [the longest x1 11.5 us: on_device(): return returned[target_device, slot_index]]
    all_to_all x2 -> x0, starting transfers between devices: 20 us -> none  [the longest x1 11.5 us: on_device(): lax.all_to_all(send_rows, ('src', 'grp'), split_axis=0, concat_axis=0, ti...]
    all_to_all x1 -> x0, blocking collectives: 17.3 us -> none  [on_device(): lax.all_to_all(answers, ('src', 'grp'), split_axis=0, concat_axis=0, tile...]
    scatter x1 -> x0, local copies, waits for them, and re-layouts: 11 us -> none  [on_device(): held_units = jnp.zeros((row_count, feature_count), jnp.bfloat16).at[got_r...]
  transfers between devices with their start and end apart: 3 -> 0, of which waited for: 3 -> 0; matrix products, arithmetic and copies ran while one was open for 4% -> 0% of each run, Pallas kernels for 0% -> 0%
where the time goes in v1:
time: 118 us
  Pallas kernels  114 us (97%)
  local copies, waits for them, and re-layouts  4.03 us (3%)
    pallas_call x1, Pallas kernels, on_device(): pl.pallas_call(kernel, out_shape=jax.ShapeDtypeStruct((1, rows), F32), in...  114 us
    unnamed x9, local copies, waits for them, and re-layouts  4.03 us

profile of v1, /device:TPU:1, one launch (start us, length us, event | category | flops | bytes accessed | tf_op | source)
XLA Modules:
  0.0 118.2 jit_solution(11910900209125198567)
XLA Ops:
  0.0 0.0 copy-start
  0.0 1.4 %copy-done = bf16[1024,768]{1,0:T(8,128)(2,1)S(1)} copy-done((bf16[1024,768]{1,0:T(8,128)(2,1)S(1)}, bf16[1024,768]{1,0:T(8,128)(2,1)}, u32[]{:S(2)}) %copy-start) | copy-done | bytes 1572888
  1.4 0.0 copy-start.1
  1.4 0.7 copy-done.1
  2.1 0.0 copy-start.2
  2.1 0.7 copy-done.2
  2.8 0.0 copy-start.3
  2.8 0.7 copy-done.3
  3.4 114.2 %dedup.1 = f32[1,1024]{1,0:T(1,128)S(1)} custom-call(bf16[1024,768]{1,0:T(8,128)(2,1)S(1)} %copy-done, s32[1,1024]{1,0:T(1,128)S(1)} %bitcast.5, s32[1,1024]{1,0:T(1,128)S(1)} %bitcast.6, s32[1,48]{1,0:T(1,128)S(1)} %bitcast.7), custom_call_target="tpu_custom_call" | custom-call | tf_op jit(solution)/shard_map/dedup/pallas_call | solution.py:382
  117.6 0.6 copy.6
Async XLA Ops:
  0.0 1.4 %copy-start = (bf16[1024,768]{1,0:T(8,128)(2,1)S(1)}, bf16[1024,768]{1,0:T(8,128)(2,1)}, u32[]{:S(2)}) copy-start(bf16[1024,768]{1,0:T(8,128)(2,1)} %embeds.1) | copy-start | bytes 4718596
  1.4 0.7 copy-start.1
  2.1 0.7 copy-start.2
  2.8 0.7 copy-start.3

commit v2 on v1

v2 whole, which is shorter than its diff:
```python
import functools

import jax
import jax.numpy as jnp
from jax import lax
from jax.experimental import pallas as pl
from jax.experimental.pallas import tpu as pltpu
from jax.sharding import PartitionSpec as P

MESH = pl.DeviceIdType.MESH
F32 = jnp.float32
BF16 = jnp.bfloat16

epsilon = 1e-06

DEVICES = 128
SRC = 16
GRP = 8
LANES = 128
SLOTS = 16
CLASSES = 4
PER = DEVICES // CLASSES
CLASS_ROWS = PER * SLOTS
HALF = 512
MIX, UNMIX = 53, 29

NN = (((1,), (0,)), ((), ()))
NT = (((1,), (1,)), ((), ()))


def dot(a, b, dims=NN):
    return lax.dot_general(a, b, dims, preferred_element_type=F32)


def one_hot(mask):
    return jnp.where(mask, 1.0, 0.0).astype(BF16)


def iota(shape, dim):
    return lax.broadcasted_iota(jnp.int32, shape, dim)


def three_parts(x):
    first = x.astype(BF16)
    rest = x - first.astype(F32)
    second = rest.astype(BF16)
    third = (rest - second.astype(F32)).astype(BF16)
    return first, second, third


def kernel(
    embeds_hbm,
    ids_hbm,
    ranks_hbm,
    sizes_hbm,
    out,
    embeds,
    ids,
    ranks,
    sizes,
    unit,
    send,
    recv,
    sent_meta,
    column_meta,
    group_meta,
    place_of,
    look,
    gathered,
    blocks,
    tops,
    lows,
    others,
    best,
    answers,
    returned,
    load_sem,
    again_sem,
    send_sem,
    recv_sem,
    column_send_sem,
    column_recv_sem,
    group_send_sem,
    group_recv_sem,
    block_send_sem,
    block_recv_sem,
    top_send_sem,
    top_recv_sem,
    answer_send_sem,
    answer_recv_sem,
):
    rows, width = embeds.shape
    src = lax.axis_index("src")
    grp = lax.axis_index("grp")
    x, y = src // 4, src % 4
    z, core = grp // 2, grp % 2

    def src_at(n, sign):
        return (x + sign * (n // 4) + 4) % 4 * 4 + (y + sign * (n % 4) + 4) % 4

    def grp_at(m, sign):
        return (z + sign * (m // 2) + 4) % 4 * 2 + (core + m % 2) % 2

    loads = []
    for n, (source, target) in enumerate(
        ((ids_hbm, ids), (ranks_hbm, ranks), (sizes_hbm, sizes), (embeds_hbm, embeds))
    ):
        copy = pltpu.make_async_copy(source, target, load_sem.at[n])
        copy.start()
        loads.append(copy)

    barrier = pltpu.get_barrier_semaphore()

    def greet_src(n, carry):
        pl.semaphore_signal(barrier, inc=1, device_id=(src_at(n, 1), grp), device_id_type=MESH)
        return carry

    def greet_grp(m, carry):
        pl.semaphore_signal(barrier, inc=1, device_id=(src, grp_at(m, 1)), device_id_type=MESH)
        return carry

    lax.fori_loop(1, SRC, greet_src, 0)
    lax.fori_loop(1, GRP, greet_grp, 0)

    for copy in loads[:3]:
        copy.wait()
    clusters = sizes.shape[1]
    size_row = sizes[...].astype(F32)
    earlier = iota((clusters, clusters), 1) < iota((clusters, clusters), 0)
    starts = jnp.sum(jnp.where(earlier, size_row, 0.0), axis=1, keepdims=True)
    mine = iota((clusters, rows), 0) == ids[...]
    start_row = jnp.sum(jnp.where(mine, starts, 0.0), axis=0, keepdims=True)
    position = start_row.astype(jnp.int32) + ranks[...]
    to_src = position >> 13
    to_grp = (position >> 10) & 7
    dx = ((to_src >> 2) - x) & 3
    dy = ((to_src & 3) - y) & 3
    dz = ((to_grp >> 1) - z) & 3
    dc = (to_grp - core) & 1
    column_row = dx * 4 + dy
    step_row = ((column_row * GRP + dz * 2 + dc) * UNMIX) & (DEVICES - 1)
    to_step = one_hot(iota((DEVICES, rows), 0) == step_row)
    to_column = one_hot(iota((SRC, rows), 0) == column_row)

    part = 256
    before = one_hot(iota((part, part), 0) < iota((part, part), 1))
    carry = jnp.zeros((DEVICES, 1), F32)
    slot_parts = []
    for n in range(rows // part):
        piece = to_step[:, n * part : (n + 1) * part]
        piece32 = piece.astype(F32)
        count = dot(piece, before) + carry
        slot_parts.append(jnp.sum(piece32 * count, axis=0, keepdims=True))
        carry = carry + jnp.sum(piece32, axis=1, keepdims=True)
    slot_row = jnp.concatenate(slot_parts, axis=1).astype(jnp.int32)
    index_row = step_row * SLOTS + slot_row
    lane_hot = one_hot(iota((LANES, rows), 0) == to_grp * SLOTS + slot_row)

    place_row = (position & (rows - 1)) + 1
    upper = to_column * (place_row >> 3).astype(F32).astype(BF16)
    lower = to_column * (place_row & 7).astype(F32).astype(BF16)
    meta = 8.0 * dot(upper, lane_hot, NT) + dot(lower, lane_hot, NT)
    for n in range(SRC):
        sent_meta[n] = meta[n : n + 1, :]
    column_meta[0] = sent_meta[0]

    pl.semaphore_wait(barrier, SRC - 1 + GRP - 1)

    def greet_again(n, carry):
        pl.semaphore_signal(again_sem, inc=1, device_id=(src_at(n, 1), grp), device_id_type=MESH)
        return carry

    lax.fori_loop(1, SRC, greet_again, 0)

    def send_column_meta(n, carry):
        pltpu.make_async_remote_copy(
            src_ref=sent_meta.at[n],
            dst_ref=column_meta.at[n],
            send_sem=column_send_sem,
            recv_sem=column_recv_sem,
            device_id=(src_at(n, 1), grp),
            device_id_type=MESH,
        ).start()
        return carry

    lax.fori_loop(1, SRC, send_column_meta, 0)

    loads[3].wait()

    def normalise(n, carry):
        here = pl.ds(pl.multiple_of(n * part, part), part)
        wide = embeds[here, :].astype(F32)
        total = jnp.sum(wide * wide, axis=1, keepdims=True)
        unit[here, :] = (wide * lax.rsqrt(total + epsilon)).astype(BF16)
        return carry

    lax.fori_loop(0, rows // part, normalise, 0)

    def wait_all(ref, sem, count):
        pltpu.make_async_copy(ref.at[pl.ds(1, count)], ref.at[pl.ds(1, count)], sem).wait()

    for n in range(CLASSES):
        pick = one_hot(iota((CLASS_ROWS, rows), 0) + n * CLASS_ROWS == index_row)
        packed = dot(pick, unit[...]).astype(BF16)
        send[pl.ds(n * PER, PER)] = packed.reshape(PER, SLOTS, width)
        if n == 0:
            recv[0] = send[0]
            pl.semaphore_wait(again_sem, SRC - 1)

        def send_step(step, carry):
            k = (step * MIX) % DEVICES
            pltpu.make_async_remote_copy(
                src_ref=send.at[step],
                dst_ref=recv.at[step],
                send_sem=send_sem.at[n],
                recv_sem=recv_sem.at[n],
                device_id=(src_at(k // GRP, 1), grp_at(k % GRP, 1)),
                device_id_type=MESH,
            ).start()
            return carry

        lax.fori_loop(max(1, n * PER), (n + 1) * PER, send_step, 0)

        if n == 0:
            wait_all(column_meta, column_recv_sem, SRC - 1)
            group_meta[0] = column_meta[...]

            def send_group_meta(m, carry):
                pltpu.make_async_remote_copy(
                    src_ref=column_meta,
                    dst_ref=group_meta.at[m],
                    send_sem=group_send_sem,
                    recv_sem=group_recv_sem,
                    device_id=(src, grp_at(m, 1)),
                    device_id_type=MESH,
                ).start()
                return carry

            lax.fori_loop(1, GRP, send_group_meta, 0)

    lane_no = iota((1, LANES), 1)
    pick_rows = []
    for n in range(SRC):
        wanted = column_meta[n].astype(jnp.int32) - 1
        look[:, n * LANES : (n + 1) * LANES] = one_hot(iota((LANES, LANES), 0) == (wanted & 127))
        row_no = (lane_no // SLOTS) * 8 + (wanted >> 7)
        pick_rows.append(jnp.where(wanted >= 0, row_no, -1))
    pick_row = jnp.concatenate(pick_rows, axis=1)

    wait_all(group_meta, group_recv_sem, GRP - 1)

    all_meta = group_meta[...].reshape(DEVICES, LANES).astype(jnp.int32)
    choose = one_hot(iota((LANES, LANES), 0) == grp * SLOTS + (iota((LANES, LANES), 1) & 15))
    number = iota((DEVICES, LANES), 0)
    step_of = (((number & 15) * GRP + (number >> 4)) * UNMIX) & (DEVICES - 1)
    kept = (iota((DEVICES, LANES), 1) >> 4) == (step_of & 7)
    number = iota((SRC, DEVICES), 1)
    step_of = (((number & 15) * GRP + (number >> 4)) * UNMIX) & (DEVICES - 1)
    line_hot = one_hot((step_of >> 3) == iota((SRC, DEVICES), 0))
    got_places = jnp.zeros((SRC, LANES), F32)
    for scale, digit in ((8.0, all_meta >> 3), (1.0, all_meta & 7)):
        spread = dot(digit.astype(F32).astype(BF16), choose)
        spread = jnp.where(kept, spread, 0.0).astype(BF16)
        got_places += scale * dot(line_hot, spread)
    got_places = got_places.astype(jnp.int32)

    for n in range(CLASSES):
        for m in range(CLASS_ROWS // LANES):
            line = n * (CLASS_ROWS // LANES) + m
            hit = iota((rows, LANES), 0) + 1 == got_places[line : line + 1, :]
            place_of[n, :, m * LANES : (m + 1) * LANES] = one_hot(hit)

    base = src * (GRP * rows)
    after, prior = (z + 1) % 4, (z + 3) % 4
    prior_core = (core + z // 2) % 2

    for half_no in range(2 * GRP):
        places = (half_no * HALF + base + iota((1, HALF), 1)).astype(F32)
        low = jnp.max(jnp.where(starts <= places, starts, 0.0), axis=0, keepdims=True)
        lows[half_no] = low.astype(jnp.int32) - base
        tops[half_no] = jnp.full((1, HALF), -1.0, F32)

    to_peer = (src, z * 2 + (core + 1) % 2)
    to_prior = (src, prior * 2 + core)
    to_after = (src, after * 2 + (core + after // 2) % 2)

    def block_copies(half):
        mine = blocks.at[core, half]
        for n, (slot, device) in enumerate(((core, to_peer), (2, to_prior), (3, to_after))):
            yield pltpu.make_async_remote_copy(
                src_ref=mine,
                dst_ref=blocks.at[slot, half],
                send_sem=block_send_sem.at[n, half],
                recv_sem=block_recv_sem.at[n, half],
                device_id=device,
                device_id_type=MESH,
            )

    for n in range(CLASSES):
        first = 1 if n == 0 else 0
        group = recv.at[pl.ds(n * PER + first, PER - first)]
        pltpu.make_async_copy(group, group, recv_sem.at[n]).wait()
        arrived = recv[pl.ds(n * PER, PER)].reshape(CLASS_ROWS, width)
        for half in range(2):
            here = pl.ds(half * HALF, HALF)
            found = dot(place_of[n, here, :], arrived)
            if n == 0:
                gathered[here, :] = found
            elif n < CLASSES - 1:
                gathered[here, :] += found
            else:
                blocks[core, half] = (gathered[here, :] + found).astype(BF16)
                for copy in block_copies(half):
                    copy.start()

    def half_of(slot, half):
        block_no = z * 2 + slot
        block_no = jnp.where(slot == 2, after * 2 + core, block_no)
        block_no = jnp.where(slot == 3, prior * 2 + prior_core, block_no)
        return block_no * 2 + half

    def score(key_slot, key_half, query_slot, query_half, same):
        products = dot(blocks[key_slot, key_half], blocks[query_slot, query_half], NT)
        line = half_of(query_slot, query_half)
        key_no = iota((HALF, HALF), 0)
        allowed = key_no >= lows[line] - half_of(key_slot, key_half) * HALF
        if same:
            allowed = allowed & (key_no < iota((HALF, HALF), 1))
        found = jnp.max(jnp.where(allowed, products, -1.0), axis=0, keepdims=True)
        tops[line] = jnp.maximum(tops[line], found)

    def score_pair(slot_a, half_a, slot_b, half_b):
        a_first = half_of(slot_a, half_a) < half_of(slot_b, half_b)
        key_slot = jnp.where(a_first, slot_a, slot_b)
        key_half = jnp.where(a_first, half_a, half_b)
        query_slot = jnp.where(a_first, slot_b, slot_a)
        query_half = jnp.where(a_first, half_b, half_a)
        score(key_slot, key_half, query_slot, query_half, False)

    def own_step(half, carry):
        score(core, half, core, half, True)
        return carry

    lax.fori_loop(0, 2, own_step, 0)

    def wait_block(n, half):
        slot = ((core + 1) % 2, 2, 3)[n]
        here = blocks.at[slot, half]
        pltpu.make_async_copy(here, here, block_recv_sem.at[n, half]).wait()

    for half in range(2):
        wait_block(0, half)

    def own_pairs(n, carry):
        plain = n == 2
        key_slot = jnp.where(plain, core, 0)
        key_half = jnp.where(plain, 0, n)
        query_slot = jnp.where(plain, core, 1)
        query_half = jnp.where(plain, 1, core)
        score(key_slot, key_half, query_slot, query_half, False)
        return carry

    lax.fori_loop(0, 3, own_pairs, 0)

    for half in range(2):
        wait_block(1, half)

        def with_after(n, carry):
            score_pair(n // 2, n % 2, 2, half)
            return carry

        lax.fori_loop(0, 4, with_after, 0)
        wait_block(2, half)

        def across(n, carry):
            number = n + half
            score_pair(3, number // 2, 2, number % 2)
            return carry

        lax.fori_loop(0, 1 + 2 * half, across, 0)

    def send_tops(m, carry):
        pltpu.make_async_remote_copy(
            src_ref=tops,
            dst_ref=others.at[m],
            send_sem=top_send_sem,
            recv_sem=top_recv_sem,
            device_id=(src, grp_at(m, 1)),
            device_id_type=MESH,
        ).start()
        return carry

    lax.fori_loop(1, GRP, send_tops, 0)
    wait_all(others, top_recv_sem, GRP - 1)
    for half_no in range(2 * GRP):
        found = tops[half_no]
        for m in range(1, GRP):
            found = jnp.maximum(found, others[m, half_no])
        for n in range(HALF // LANES):
            line = half_no * (HALF // LANES) + n
            best[line : line + 1, :] = found[:, n * LANES : (n + 1) * LANES]

    answer = jnp.zeros((best.shape[0], SRC * LANES), F32)
    for piece in three_parts(best[...]):
        answer += dot(piece, look[...])
    right = iota(answer.shape, 0) == pick_row
    answer = jnp.sum(jnp.where(right, answer, 0.0), axis=0, keepdims=True)
    for n in range(SRC):
        answers[n] = answer[:, n * LANES : (n + 1) * LANES]
    returned[0] = answers[0]

    def send_answer(n, carry):
        pltpu.make_async_remote_copy(
            src_ref=answers.at[n],
            dst_ref=returned.at[n],
            send_sem=answer_send_sem,
            recv_sem=answer_recv_sem,
            device_id=(src_at(n, -1), grp),
            device_id_type=MESH,
        ).start()
        return carry

    lax.fori_loop(1, SRC, send_answer, 0)
    wait_all(returned, answer_recv_sem, SRC - 1)
    table = returned[...].reshape(SRC, LANES).T
    chosen = jnp.zeros((LANES, rows), F32)
    for piece in three_parts(table):
        chosen += dot(piece, to_column)
    out[...] = jnp.sum(chosen * lane_hot.astype(F32), axis=0, keepdims=True)

    wait_all(sent_meta, column_send_sem, SRC - 1)
    wait_all(group_meta, group_send_sem, GRP - 1)
    wait_all(others, top_send_sem, GRP - 1)
    wait_all(answers, answer_send_sem, SRC - 1)
    for n in range(CLASSES):
        first = 1 if n == 0 else 0
        group = send.at[pl.ds(n * PER + first, PER - first)]
        pltpu.make_async_copy(group, group, send_sem.at[n]).wait()
    for n in range(3):
        for half in range(2):
            here = blocks.at[core, half]
            pltpu.make_async_copy(here, here, block_send_sem.at[n, half]).wait()


def on_device(embeds, cluster_id, cluster_rank, cluster_size):
    rows, width = embeds.shape
    clusters = cluster_size.shape[0]
    best = pl.pallas_call(
        kernel,
        out_shape=jax.ShapeDtypeStruct((1, rows), F32),
        in_specs=[pl.BlockSpec(memory_space=pl.ANY)] * 4,
        out_specs=pl.BlockSpec(memory_space=pltpu.VMEM),
        scratch_shapes=[
            pltpu.VMEM((rows, width), BF16),
            pltpu.VMEM((1, rows), jnp.int32),
            pltpu.VMEM((1, rows), jnp.int32),
            pltpu.VMEM((1, clusters), jnp.int32),
            pltpu.VMEM((rows, width), BF16),
            pltpu.VMEM((DEVICES, SLOTS, width), BF16),
            pltpu.VMEM((DEVICES, SLOTS, width), BF16),
            pltpu.VMEM((SRC, 1, LANES), F32),
            pltpu.VMEM((SRC, 1, LANES), F32),
            pltpu.VMEM((GRP, SRC, 1, LANES), F32),
            pltpu.VMEM((CLASSES, rows, CLASS_ROWS), BF16),
            pltpu.VMEM((LANES, SRC * LANES), BF16),
            pltpu.VMEM((rows, width), F32),
            pltpu.VMEM((4, 2, HALF, width), BF16),
            pltpu.VMEM((2 * GRP, 1, HALF), F32),
            pltpu.VMEM((2 * GRP, 1, HALF), jnp.int32),
            pltpu.VMEM((GRP, 2 * GRP, 1, HALF), F32),
            pltpu.VMEM((GRP * rows // LANES, LANES), F32),
            pltpu.VMEM((SRC, 1, LANES), F32),
            pltpu.VMEM((SRC, 1, LANES), F32),
            pltpu.SemaphoreType.DMA((4,)),
            pltpu.SemaphoreType.REGULAR,
            pltpu.SemaphoreType.DMA((CLASSES,)),
            pltpu.SemaphoreType.DMA((CLASSES,)),
            pltpu.SemaphoreType.DMA,
            pltpu.SemaphoreType.DMA,
            pltpu.SemaphoreType.DMA,
            pltpu.SemaphoreType.DMA,
            pltpu.SemaphoreType.DMA((3, 2)),
            pltpu.SemaphoreType.DMA((3, 2)),
            pltpu.SemaphoreType.DMA,
            pltpu.SemaphoreType.DMA,
            pltpu.SemaphoreType.DMA,
            pltpu.SemaphoreType.DMA,
        ],
        compiler_params=pltpu.CompilerParams(
            collective_id=0, has_side_effects=True, vmem_limit_bytes=50 * 1024 * 1024
        ),
        name="dedup",
    )(
        embeds,
        cluster_id.reshape(1, rows),
        cluster_rank.reshape(1, rows),
        cluster_size.reshape(1, -1),
    )
    return best.reshape(rows)


def solution(mesh):
    placed = (P(("src", "grp"), None), P(("src", "grp")), P(("src", "grp")), P())
    return jax.shard_map(
        on_device, mesh=mesh, in_specs=placed, out_specs=P(("src", "grp")), check_vma=False
    )
```

time: 118 us -> 105 us (0.89)
  Pallas kernels: 114 us -> 101 us
    pallas_call x1, Pallas kernels: 114 us -> 101 us  [on_device(): pl.pallas_call(kernel, out_shape=jax.ShapeDtypeStruct((1, rows), F32), in...]
where the time goes in v2:
time: 105 us
  Pallas kernels  101 us (96%)
  local copies, waits for them, and re-layouts  4.03 us (4%)
    pallas_call x1, Pallas kernels, on_device(): pl.pallas_call(kernel, out_shape=jax.ShapeDtypeStruct((1, rows), F32), in...  101 us
    unnamed x9, local copies, waits for them, and re-layouts  4.03 us

profile of v2, /device:TPU:1, one launch (start us, length us, event | category | flops | bytes accessed | tf_op | source)
XLA Modules:
  0.0 105.2 jit_solution(1630267281044434273)
XLA Ops:
  0.0 0.0 copy-start
  0.0 1.4 %copy-done = bf16[1024,768]{1,0:T(8,128)(2,1)S(1)} copy-done((bf16[1024,768]{1,0:T(8,128)(2,1)S(1)}, bf16[1024,768]{1,0:T(8,128)(2,1)}, u32[]{:S(2)}) %copy-start) | copy-done | bytes 1572888
  1.4 0.0 copy-start.1
  1.4 0.7 copy-done.1
  2.1 0.0 copy-start.2
  2.1 0.7 copy-done.2
  2.8 0.0 copy-start.3
  2.8 0.7 copy-done.3
  3.4 101.2 %dedup.1 = f32[1,1024]{1,0:T(1,128)S(1)} custom-call(bf16[1024,768]{1,0:T(8,128)(2,1)S(1)} %copy-done, s32[1,1024]{1,0:T(1,128)S(1)} %bitcast.5, s32[1,1024]{1,0:T(1,128)S(1)} %bitcast.6, s32[1,48]{1,0:T(1,128)S(1)} %bitcast.7), custom_call_target="tpu_custom_call" | custom-call | tf_op jit(solution)/shard_map/dedup/pallas_call | solution.py:448
  104.6 0.6 copy.6
Async XLA Ops:
  0.0 1.4 %copy-start = (bf16[1024,768]{1,0:T(8,128)(2,1)S(1)}, bf16[1024,768]{1,0:T(8,128)(2,1)}, u32[]{:S(2)}) copy-start(bf16[1024,768]{1,0:T(8,128)(2,1)} %embeds_hbm.1) | copy-start | bytes 4718596
  1.4 0.7 copy-start.1
  2.1 0.7 copy-start.2
  2.8 0.7 copy-start.3

commit v3 on v2

--- a/solution.py
+++ b/solution.py
@@ -1,5 +1,3 @@
-import functools
-
 import jax
 import jax.numpy as jnp
 from jax import lax
@@ -22,6 +20,8 @@
 PER = DEVICES // CLASSES
 CLASS_ROWS = PER * SLOTS
 HALF = 512
+QUARTER = 256
+HELD = 6
 MIX, UNMIX = 53, 29
 
 NN = (((1,), (0,)), ((), ()))
@@ -71,6 +71,7 @@
     tops,
     lows,
     others,
+    own_best,
     best,
     answers,
     returned,
@@ -84,8 +85,14 @@
     group_recv_sem,
     block_send_sem,
     block_recv_sem,
+    peer_send_sem,
+    peer_recv_sem,
+    forward_send_sem,
+    forward_recv_sem,
     top_send_sem,
     top_recv_sem,
+    best_send_sem,
+    best_recv_sem,
     answer_send_sem,
     answer_recv_sem,
 ):
@@ -131,12 +138,14 @@
     mine = iota((clusters, rows), 0) == ids[...]
     start_row = jnp.sum(jnp.where(mine, starts, 0.0), axis=0, keepdims=True)
     position = start_row.astype(jnp.int32) + ranks[...]
-    to_src = position >> 13
-    to_grp = (position >> 10) & 7
-    dx = ((to_src >> 2) - x) & 3
-    dy = ((to_src & 3) - y) & 3
-    dz = ((to_grp >> 1) - z) & 3
-    dc = (to_grp - core) & 1
+    tiling = position >> 16
+    to_x = (((position >> 15) & 1) * 2 + ((position >> 12) & 1) - tiling) & 3
+    to_y = (((position >> 14) & 1) * 2 + ((position >> 11) & 1) - tiling) & 3
+    to_z = (((position >> 13) & 1) * 2 + ((position >> 10) & 1) - tiling) & 3
+    to_core = (position >> 9) & 1
+    to_grp = to_z * 2 + to_core
+    dx, dy, dz = (to_x - x) & 3, (to_y - y) & 3, (to_z - z) & 3
+    dc = (to_core - core) & 1
     column_row = dx * 4 + dy
     step_row = ((column_row * GRP + dz * 2 + dc) * UNMIX) & (DEVICES - 1)
     to_step = one_hot(iota((DEVICES, rows), 0) == step_row)
@@ -156,7 +165,7 @@
     index_row = step_row * SLOTS + slot_row
     lane_hot = one_hot(iota((LANES, rows), 0) == to_grp * SLOTS + slot_row)
 
-    place_row = (position & (rows - 1)) + 1
+    place_row = tiling * HALF + (position & (HALF - 1)) + 1
     upper = to_column * (place_row >> 3).astype(F32).astype(BF16)
     lower = to_column * (place_row & 7).astype(F32).astype(BF16)
     meta = 8.0 * dot(upper, lane_hot, NT) + dot(lower, lane_hot, NT)
@@ -270,138 +279,248 @@
             hit = iota((rows, LANES), 0) + 1 == got_places[line : line + 1, :]
             place_of[n, :, m * LANES : (m + 1) * LANES] = one_hot(hit)
 
-    base = src * (GRP * rows)
-    after, prior = (z + 1) % 4, (z + 3) % 4
-    prior_core = (core + z // 2) % 2
-
-    for half_no in range(2 * GRP):
-        places = (half_no * HALF + base + iota((1, HALF), 1)).astype(F32)
-        low = jnp.max(jnp.where(starts <= places, starts, 0.0), axis=0, keepdims=True)
-        lows[half_no] = low.astype(jnp.int32) - base
-        tops[half_no] = jnp.full((1, HALF), -1.0, F32)
-
-    to_peer = (src, z * 2 + (core + 1) % 2)
-    to_prior = (src, prior * 2 + core)
-    to_after = (src, after * 2 + (core + after // 2) % 2)
-
-    def block_copies(half):
-        mine = blocks.at[core, half]
-        for n, (slot, device) in enumerate(((core, to_peer), (2, to_prior), (3, to_after))):
-            yield pltpu.make_async_remote_copy(
-                src_ref=mine,
-                dst_ref=blocks.at[slot, half],
-                send_sem=block_send_sem.at[n, half],
-                recv_sem=block_recv_sem.at[n, half],
-                device_id=device,
-                device_id_type=MESH,
-            )
+    def bits(tiling):
+        return (x + tiling) % 2, (y + tiling) % 2, (z + tiling) % 2
+
+    def across(tiling, *axes):
+        place = [x, y, z]
+        for axis in axes:
+            place[axis] = (place[axis] + 1 - 2 * bits(tiling)[axis] + 4) % 4
+        return place
+
+    def device_across(tiling, axes, to_core):
+        to_x, to_y, to_z = across(tiling, *axes)
+        return (to_x * 4 + to_y, to_z * 2 + to_core)
+
+    def number(tiling, slot):
+        v1, v2, v3 = bits(tiling)
+        if not isinstance(slot, int) or slot < 2:
+            own = slot
+        elif slot == 2:
+            v1, own = 1 - v1, (core + v1) % 2
+        elif slot == 3:
+            v2, own = 1 - v2, core
+        elif slot == 4:
+            v3, own = 1 - v3, (core + v2) % 2
+        else:
+            v2, v3, own = 1 - v2, 1 - v3, core
+        return ((v1 * 2 + v2) * 2 + v3) * 2 + own
+
+    def base(tiling):
+        cube_x, cube_y, cube_z = ((i + tiling) % 4 // 2 for i in (x, y, z))
+        return (tiling * 8 + cube_x * 4 + cube_y * 2 + cube_z) * (GRP * rows)
+
+    for tiling in range(2):
+        for slot in range(HELD):
+            places = number(tiling, slot) * HALF + base(tiling) + iota((1, HALF), 1)
+            below = jnp.where(starts <= places.astype(F32), starts, 0.0)
+            low = jnp.max(below, axis=0, keepdims=True)
+            lows[tiling, slot] = low.astype(jnp.int32) - base(tiling)
+            tops[tiling, slot] = jnp.full((1, HALF), -1.0, F32)
+
+    def first_half(axis):
+        return 1 if axis == 1 else 0
+
+    def neighbour_copy(tiling, axis, half):
+        v1, v2, v3 = bits(tiling)
+        to_core = (core + (1 - v1, 0, v2)[axis]) % 2
+        here = pl.ds(half * QUARTER, QUARTER)
+        return pltpu.make_async_remote_copy(
+            src_ref=blocks.at[tiling, core, here],
+            dst_ref=blocks.at[tiling, 2 + axis, here],
+            send_sem=block_send_sem.at[tiling, axis, half],
+            recv_sem=block_recv_sem.at[tiling, axis, half],
+            device_id=device_across(tiling, (axis,), to_core),
+            device_id_type=MESH,
+        )
+
+    def peer_copy(tiling):
+        return pltpu.make_async_remote_copy(
+            src_ref=blocks.at[tiling, core],
+            dst_ref=blocks.at[tiling, core],
+            send_sem=peer_send_sem.at[tiling],
+            recv_sem=peer_recv_sem.at[tiling],
+            device_id=(src, z * 2 + (core + 1) % 2),
+            device_id_type=MESH,
+        )
+
+    def forward_copy(tiling, axis):
+        half = first_half(axis)
+        here = pl.ds(half * QUARTER, QUARTER)
+        to_core = core if axis == 1 else (core + bits(tiling)[1]) % 2
+        return pltpu.make_async_remote_copy(
+            src_ref=blocks.at[tiling, 2 + axis, here],
+            dst_ref=blocks.at[tiling, 5, here],
+            send_sem=forward_send_sem.at[tiling, half],
+            recv_sem=forward_recv_sem.at[tiling, half],
+            device_id=device_across(tiling, (3 - axis,), to_core),
+            device_id_type=MESH,
+        )
 
     for n in range(CLASSES):
         first = 1 if n == 0 else 0
         group = recv.at[pl.ds(n * PER + first, PER - first)]
         pltpu.make_async_copy(group, group, recv_sem.at[n]).wait()
         arrived = recv[pl.ds(n * PER, PER)].reshape(CLASS_ROWS, width)
-        for half in range(2):
-            here = pl.ds(half * HALF, HALF)
+        for tiling in range(2):
+            here = pl.ds(tiling * HALF, HALF)
             found = dot(place_of[n, here, :], arrived)
             if n == 0:
                 gathered[here, :] = found
             elif n < CLASSES - 1:
                 gathered[here, :] += found
             else:
-                blocks[core, half] = (gathered[here, :] + found).astype(BF16)
-                for copy in block_copies(half):
-                    copy.start()
-
-    def half_of(slot, half):
-        block_no = z * 2 + slot
-        block_no = jnp.where(slot == 2, after * 2 + core, block_no)
-        block_no = jnp.where(slot == 3, prior * 2 + prior_core, block_no)
-        return block_no * 2 + half
-
-    def score(key_slot, key_half, query_slot, query_half, same):
-        products = dot(blocks[key_slot, key_half], blocks[query_slot, query_half], NT)
-        line = half_of(query_slot, query_half)
-        key_no = iota((HALF, HALF), 0)
-        allowed = key_no >= lows[line] - half_of(key_slot, key_half) * HALF
+                blocks[tiling, core] = (gathered[here, :] + found).astype(BF16)
+                for axis in range(3):
+                    neighbour_copy(tiling, axis, first_half(axis)).start()
+                peer_copy(tiling).start()
+                for axis in range(3):
+                    neighbour_copy(tiling, axis, 1 - first_half(axis)).start()
+
+    def score(tiling, key, query, same=False):
+        key_slot, key_start, keys = key[:3]
+        query_slot, query_start, queries = query[:3]
+        products = dot(
+            blocks[tiling, key_slot, pl.ds(key_start, keys), :],
+            blocks[tiling, query_slot, pl.ds(query_start, queries), :],
+            NT,
+        )
+        columns = slice(query_start, query_start + queries)
+        key_no = iota((keys, queries), 0) + key_start
+        allowed = key_no >= lows[tiling, query_slot][:, columns] - key[3] * HALF
         if same:
-            allowed = allowed & (key_no < iota((HALF, HALF), 1))
+            allowed = allowed & (key_no < iota((keys, queries), 1) + query_start)
         found = jnp.max(jnp.where(allowed, products, -1.0), axis=0, keepdims=True)
-        tops[line] = jnp.maximum(tops[line], found)
-
-    def score_pair(slot_a, half_a, slot_b, half_b):
-        a_first = half_of(slot_a, half_a) < half_of(slot_b, half_b)
-        key_slot = jnp.where(a_first, slot_a, slot_b)
-        key_half = jnp.where(a_first, half_a, half_b)
-        query_slot = jnp.where(a_first, slot_b, slot_a)
-        query_half = jnp.where(a_first, half_b, half_a)
-        score(key_slot, key_half, query_slot, query_half, False)
-
-    def own_step(half, carry):
-        score(core, half, core, half, True)
-        return carry
-
-    lax.fori_loop(0, 2, own_step, 0)
-
-    def wait_block(n, half):
-        slot = ((core + 1) % 2, 2, 3)[n]
-        here = blocks.at[slot, half]
-        pltpu.make_async_copy(here, here, block_recv_sem.at[n, half]).wait()
-
-    for half in range(2):
-        wait_block(0, half)
-
-    def own_pairs(n, carry):
-        plain = n == 2
-        key_slot = jnp.where(plain, core, 0)
-        key_half = jnp.where(plain, 0, n)
-        query_slot = jnp.where(plain, core, 1)
-        query_half = jnp.where(plain, 1, core)
-        score(key_slot, key_half, query_slot, query_half, False)
-        return carry
-
-    lax.fori_loop(0, 3, own_pairs, 0)
-
-    for half in range(2):
-        wait_block(1, half)
-
-        def with_after(n, carry):
-            score_pair(n // 2, n % 2, 2, half)
-            return carry
-
-        lax.fori_loop(0, 4, with_after, 0)
-        wait_block(2, half)
-
-        def across(n, carry):
-            number = n + half
-            score_pair(3, number // 2, 2, number % 2)
-            return carry
-
-        lax.fori_loop(0, 1 + 2 * half, across, 0)
-
-    def send_tops(m, carry):
+        tops[tiling, query_slot, :, columns] = jnp.maximum(
+            tops[tiling, query_slot, :, columns], found
+        )
+
+    def pair(tiling, a, b):
+        a, b = (*a, number(tiling, a[0])), (*b, number(tiling, b[0]))
+        a_first = a[3] < b[3]
+
+        @pl.when(a_first)
+        def _():
+            score(tiling, a, b)
+
+        @pl.when(jnp.logical_not(a_first))
+        def _():
+            score(tiling, b, a)
+
+    def own_slot(tiling, axis):
+        v1, v2, v3 = bits(tiling)
+        return (core + (0, v2, v2 + v3)[axis]) % 2
+
+    def own_scores(tiling, carry):
+        mine = (core, 0, HALF, number(tiling, core))
+        score(tiling, mine, mine, True)
+        peer = blocks.at[tiling, (core + 1) % 2]
+        pltpu.make_async_copy(peer, peer, peer_recv_sem.at[tiling]).wait()
+        start = pl.multiple_of(core * QUARTER, QUARTER)
+        key = (0, start, QUARTER, number(tiling, 0))
+        score(tiling, key, (1, 0, HALF, number(tiling, 1)))
+        return carry
+
+    lax.fori_loop(0, 2, own_scores, 0)
+
+    def wait_neighbour(tiling, axis, half):
+        here = blocks.at[tiling, 2 + axis, pl.ds(half * QUARTER, QUARTER)]
+        pltpu.make_async_copy(here, here, block_recv_sem.at[tiling, axis, half]).wait()
+
+    def forward(tiling, carry):
+        for axis in (1, 2):
+            wait_neighbour(tiling, axis, first_half(axis))
+            forward_copy(tiling, axis).start()
+        return carry
+
+    lax.fori_loop(0, 2, forward, 0)
+
+    def held_part(axis, half):
+        return (2 + axis, half * QUARTER, QUARTER)
+
+    def first_scores(tiling, carry):
+        wait_neighbour(tiling, 0, first_half(0))
+        for axis in range(3):
+            own = (own_slot(tiling, axis), 0, HALF)
+            pair(tiling, own, held_part(axis, first_half(axis)))
+        for axis, other in ((0, 1), (0, 2), (1, 2)):
+            pair(
+                tiling, held_part(axis, first_half(axis)), held_part(other, first_half(other))
+            )
+        return carry
+
+    lax.fori_loop(0, 2, first_scores, 0)
+
+    def second_scores(tiling, carry):
+        for axis in range(3):
+            wait_neighbour(tiling, axis, 1 - first_half(axis))
+            own = (own_slot(tiling, axis), 0, HALF)
+            pair(tiling, own, held_part(axis, 1 - first_half(axis)))
+        for axis, other in ((0, 1), (0, 2), (1, 2)):
+            pair(tiling, held_part(axis, 1 - first_half(axis)), (2 + other, 0, HALF))
+            pair(
+                tiling,
+                held_part(axis, first_half(axis)),
+                held_part(other, 1 - first_half(other)),
+            )
+        return carry
+
+    lax.fori_loop(0, 2, second_scores, 0)
+
+    def far_scores(tiling, carry):
+        for half in range(2):
+            here = blocks.at[tiling, 5, pl.ds(half * QUARTER, QUARTER)]
+            pltpu.make_async_copy(here, here, forward_recv_sem.at[tiling, half]).wait()
+            pair(tiling, (2, 0, HALF), (5, half * QUARTER, QUARTER))
+        return carry
+
+    lax.fori_loop(0, 2, far_scores, 0)
+
+    for tiling in range(2):
+        v1, v2, v3 = bits(tiling)
+        targets = (
+            ((core + 1) % 2, (), (core + 1) % 2),
+            (2, (0,), (core + v1) % 2),
+            (3, (1,), core),
+            (4, (2,), (core + v2) % 2),
+            (5, (1, 2), core),
+        )
+        for n, (slot, axes, to_core) in enumerate(targets):
+            pltpu.make_async_remote_copy(
+                src_ref=tops.at[tiling, slot],
+                dst_ref=others.at[tiling * 5 + n],
+                send_sem=top_send_sem,
+                recv_sem=top_recv_sem,
+                device_id=device_across(tiling, axes, to_core),
+                device_id_type=MESH,
+            ).start()
+    pltpu.make_async_copy(others, others, top_recv_sem).wait()
+    for tiling in range(2):
+        found = tops[tiling, core]
+        for n in range(5):
+            found = jnp.maximum(found, others[tiling * 5 + n])
+        for n in range(HALF // LANES):
+            line = tiling * (HALF // LANES) + n
+            own_best[line : line + 1, :] = found[:, n * LANES : (n + 1) * LANES]
+
+    best[grp] = own_best[...]
+
+    def send_best(m, carry):
         pltpu.make_async_remote_copy(
-            src_ref=tops,
-            dst_ref=others.at[m],
-            send_sem=top_send_sem,
-            recv_sem=top_recv_sem,
+            src_ref=own_best,
+            dst_ref=best.at[grp],
+            send_sem=best_send_sem,
+            recv_sem=best_recv_sem,
             device_id=(src, grp_at(m, 1)),
             device_id_type=MESH,
         ).start()
         return carry
 
-    lax.fori_loop(1, GRP, send_tops, 0)
-    wait_all(others, top_recv_sem, GRP - 1)
-    for half_no in range(2 * GRP):
-        found = tops[half_no]
-        for m in range(1, GRP):
-            found = jnp.maximum(found, others[m, half_no])
-        for n in range(HALF // LANES):
-            line = half_no * (HALF // LANES) + n
-            best[line : line + 1, :] = found[:, n * LANES : (n + 1) * LANES]
-
-    answer = jnp.zeros((best.shape[0], SRC * LANES), F32)
-    for piece in three_parts(best[...]):
+    lax.fori_loop(1, GRP, send_best, 0)
+    wait_all(best, best_recv_sem, GRP - 1)
+
+    answer = jnp.zeros((GRP * rows // LANES, SRC * LANES), F32)
+    for piece in three_parts(best[...].reshape(GRP * rows // LANES, LANES)):
         answer += dot(piece, look[...])
     right = iota(answer.shape, 0) == pick_row
     answer = jnp.sum(jnp.where(right, answer, 0.0), axis=0, keepdims=True)
@@ -430,16 +549,21 @@
 
     wait_all(sent_meta, column_send_sem, SRC - 1)
     wait_all(group_meta, group_send_sem, GRP - 1)
-    wait_all(others, top_send_sem, GRP - 1)
+    pltpu.make_async_copy(others, others, top_send_sem).wait()
+    wait_all(best, best_send_sem, GRP - 1)
     wait_all(answers, answer_send_sem, SRC - 1)
     for n in range(CLASSES):
         first = 1 if n == 0 else 0
         group = send.at[pl.ds(n * PER + first, PER - first)]
         pltpu.make_async_copy(group, group, send_sem.at[n]).wait()
-    for n in range(3):
+    for tiling in range(2):
+        whole = blocks.at[tiling, core]
+        pltpu.make_async_copy(whole, whole, peer_send_sem.at[tiling]).wait()
         for half in range(2):
-            here = blocks.at[core, half]
-            pltpu.make_async_copy(here, here, block_send_sem.at[n, half]).wait()
+            here = blocks.at[tiling, core, pl.ds(half * QUARTER, QUARTER)]
+            for axis in range(3):
+                pltpu.make_async_copy(here, here, block_send_sem.at[tiling, axis, half]).wait()
+            pltpu.make_async_copy(here, here, forward_send_sem.at[tiling, half]).wait()
 
 
 def on_device(embeds, cluster_id, cluster_rank, cluster_size):
@@ -464,11 +588,12 @@
             pltpu.VMEM((CLASSES, rows, CLASS_ROWS), BF16),
             pltpu.VMEM((LANES, SRC * LANES), BF16),
             pltpu.VMEM((rows, width), F32),
-            pltpu.VMEM((4, 2, HALF, width), BF16),
-            pltpu.VMEM((2 * GRP, 1, HALF), F32),
-            pltpu.VMEM((2 * GRP, 1, HALF), jnp.int32),
-            pltpu.VMEM((GRP, 2 * GRP, 1, HALF), F32),
-            pltpu.VMEM((GRP * rows // LANES, LANES), F32),
+            pltpu.VMEM((2, HELD, HALF, width), BF16),
+            pltpu.VMEM((2, HELD, 1, HALF), F32),
+            pltpu.VMEM((2, HELD, 1, HALF), jnp.int32),
+            pltpu.VMEM((2 * (HELD - 1), 1, HALF), F32),
+            pltpu.VMEM((rows // LANES, LANES), F32),
+            pltpu.VMEM((GRP, rows // LANES, LANES), F32),
             pltpu.VMEM((SRC, 1, LANES), F32),
             pltpu.VMEM((SRC, 1, LANES), F32),
             pltpu.SemaphoreType.DMA((4,)),
@@ -479,8 +604,14 @@
             pltpu.SemaphoreType.DMA,
             pltpu.SemaphoreType.DMA,
             pltpu.SemaphoreType.DMA,
-            pltpu.SemaphoreType.DMA((3, 2)),
-            pltpu.SemaphoreType.DMA((3, 2)),
+            pltpu.SemaphoreType.DMA((2, 3, 2)),
+            pltpu.SemaphoreType.DMA((2, 3, 2)),
+            pltpu.SemaphoreType.DMA((2,)),
+            pltpu.SemaphoreType.DMA((2,)),
+            pltpu.SemaphoreType.DMA((2, 2)),
+            pltpu.SemaphoreType.DMA((2, 2)),
+            pltpu.SemaphoreType.DMA,
+            pltpu.SemaphoreType.DMA,
             pltpu.SemaphoreType.DMA,
             pltpu.SemaphoreType.DMA,
             pltpu.SemaphoreType.DMA,

time: 105 us -> 96.5 us (0.919)
  Pallas kernels: 101 us -> 92.2 us
    pallas_call x1, Pallas kernels: 101 us -> 92.2 us  [on_device(): pl.pallas_call(kernel, out_shape=jax.ShapeDtypeStruct((1, rows), F32), in...]
where the time goes in v3:
time: 96.5 us; the launch traced here: 96.3 us
  Pallas kernels  92.2 us (96%)
  local copies, waits for them, and re-layouts  4.03 us (4%)
    pallas_call x1, Pallas kernels, on_device(): pl.pallas_call(kernel, out_shape=jax.ShapeDtypeStruct((1, rows), F32), in...  92.2 us
    unnamed x9, local copies, waits for them, and re-layouts  4.03 us

profile of v3, /device:TPU:1, one launch (start us, length us, event | category | flops | bytes accessed | tf_op | source)
XLA Modules:
  0.0 96.3 jit_solution(14937762792823983525)
XLA Ops:
  0.0 0.0 copy-start
  0.0 1.4 %copy-done = bf16[1024,768]{1,0:T(8,128)(2,1)S(1)} copy-done((bf16[1024,768]{1,0:T(8,128)(2,1)S(1)}, bf16[1024,768]{1,0:T(8,128)(2,1)}, u32[]{:S(2)}) %copy-start) | copy-done | bytes 1572888
  1.4 0.0 copy-start.1
  1.4 0.7 copy-done.1
  2.1 0.0 copy-start.2
  2.1 0.7 copy-done.2
  2.8 0.0 copy-start.3
  2.8 0.7 copy-done.3
  3.4 92.2 %dedup.1 = f32[1,1024]{1,0:T(1,128)S(1)} custom-call(bf16[1024,768]{1,0:T(8,128)(2,1)S(1)} %copy-done, s32[1,1024]{1,0:T(1,128)S(1)} %bitcast.5, s32[1,1024]{1,0:T(1,128)S(1)} %bitcast.6, s32[1,48]{1,0:T(1,128)S(1)} %bitcast.7), custom_call_target="tpu_custom_call" | custom-call | tf_op jit(solution)/shard_map/dedup/pallas_call | solution.py:572
  95.7 0.6 copy.6
Async XLA Ops:
  0.0 1.4 %copy-start = (bf16[1024,768]{1,0:T(8,128)(2,1)S(1)}, bf16[1024,768]{1,0:T(8,128)(2,1)}, u32[]{:S(2)}) copy-start(bf16[1024,768]{1,0:T(8,128)(2,1)} %embeds_hbm.1) | copy-start | bytes 4718596
  1.4 0.7 copy-start.1
  2.1 0.7 copy-start.2
  2.8 0.7 copy-start.3

commit v4 on v3

--- a/solution.py
+++ b/solution.py
@@ -22,6 +22,7 @@
 HALF = 512
 QUARTER = 256
 HELD = 6
+EARLY = 58
 MIX, UNMIX = 53, 29
 
 NN = (((1,), (0,)), ((), ()))
@@ -70,8 +71,9 @@
     blocks,
     tops,
     lows,
-    others,
-    own_best,
+    shares,
+    early,
+    late,
     best,
     answers,
     returned,
@@ -89,24 +91,24 @@
     peer_recv_sem,
     forward_send_sem,
     forward_recv_sem,
-    top_send_sem,
-    top_recv_sem,
-    best_send_sem,
-    best_recv_sem,
+    early_send_sem,
+    early_recv_sem,
+    late_send_sem,
+    late_recv_sem,
     answer_send_sem,
     answer_recv_sem,
 ):
     rows, width = embeds.shape
     src = lax.axis_index("src")
     grp = lax.axis_index("grp")
-    x, y = src // 4, src % 4
-    z, core = grp // 2, grp % 2
+    x, y = src >> 2, src & 3
+    z, core = grp >> 1, grp & 1
 
     def src_at(n, sign):
-        return (x + sign * (n // 4) + 4) % 4 * 4 + (y + sign * (n % 4) + 4) % 4
+        return ((x + sign * (n >> 2)) & 3) * 4 + ((y + sign * n) & 3)
 
     def grp_at(m, sign):
-        return (z + sign * (m // 2) + 4) % 4 * 2 + (core + m % 2) % 2
+        return ((z + sign * (m >> 1)) & 3) * 2 + ((core + m) & 1)
 
     loads = []
     for n, (source, target) in enumerate(
@@ -175,11 +177,11 @@
 
     pl.semaphore_wait(barrier, SRC - 1 + GRP - 1)
 
-    def greet_again(n, carry):
-        pl.semaphore_signal(again_sem, inc=1, device_id=(src_at(n, 1), grp), device_id_type=MESH)
-        return carry
-
-    lax.fori_loop(1, SRC, greet_again, 0)
+    def greet_again(m, carry):
+        pl.semaphore_signal(again_sem, inc=1, device_id=(src, grp_at(m, 1)), device_id_type=MESH)
+        return carry
+
+    lax.fori_loop(1, GRP, greet_again, 0)
 
     def send_column_meta(n, carry):
         pltpu.make_async_remote_copy(
@@ -214,16 +216,16 @@
         send[pl.ds(n * PER, PER)] = packed.reshape(PER, SLOTS, width)
         if n == 0:
             recv[0] = send[0]
-            pl.semaphore_wait(again_sem, SRC - 1)
+            pl.semaphore_wait(again_sem, GRP - 1)
 
         def send_step(step, carry):
-            k = (step * MIX) % DEVICES
+            k = (step * MIX) & (DEVICES - 1)
             pltpu.make_async_remote_copy(
                 src_ref=send.at[step],
                 dst_ref=recv.at[step],
                 send_sem=send_sem.at[n],
                 recv_sem=recv_sem.at[n],
-                device_id=(src_at(k // GRP, 1), grp_at(k % GRP, 1)),
+                device_id=(src_at(k >> 3, 1), grp_at(k & 7, 1)),
                 device_id_type=MESH,
             ).start()
             return carry
@@ -280,12 +282,12 @@
             place_of[n, :, m * LANES : (m + 1) * LANES] = one_hot(hit)
 
     def bits(tiling):
-        return (x + tiling) % 2, (y + tiling) % 2, (z + tiling) % 2
+        return (x + tiling) & 1, (y + tiling) & 1, (z + tiling) & 1
 
     def across(tiling, *axes):
         place = [x, y, z]
         for axis in axes:
-            place[axis] = (place[axis] + 1 - 2 * bits(tiling)[axis] + 4) % 4
+            place[axis] = (place[axis] + 1 - 2 * bits(tiling)[axis]) & 3
         return place
 
     def device_across(tiling, axes, to_core):
@@ -297,17 +299,17 @@
         if not isinstance(slot, int) or slot < 2:
             own = slot
         elif slot == 2:
-            v1, own = 1 - v1, (core + v1) % 2
+            v1, own = 1 - v1, core ^ v1
         elif slot == 3:
             v2, own = 1 - v2, core
         elif slot == 4:
-            v3, own = 1 - v3, (core + v2) % 2
+            v3, own = 1 - v3, core ^ v2
         else:
             v2, v3, own = 1 - v2, 1 - v3, core
         return ((v1 * 2 + v2) * 2 + v3) * 2 + own
 
     def base(tiling):
-        cube_x, cube_y, cube_z = ((i + tiling) % 4 // 2 for i in (x, y, z))
+        cube_x, cube_y, cube_z = (((i + tiling) & 3) >> 1 for i in (x, y, z))
         return (tiling * 8 + cube_x * 4 + cube_y * 2 + cube_z) * (GRP * rows)
 
     for tiling in range(2):
@@ -323,7 +325,7 @@
 
     def neighbour_copy(tiling, axis, half):
         v1, v2, v3 = bits(tiling)
-        to_core = (core + (1 - v1, 0, v2)[axis]) % 2
+        to_core = core ^ (1 - v1, 0, v2)[axis]
         here = pl.ds(half * QUARTER, QUARTER)
         return pltpu.make_async_remote_copy(
             src_ref=blocks.at[tiling, core, here],
@@ -340,14 +342,14 @@
             dst_ref=blocks.at[tiling, core],
             send_sem=peer_send_sem.at[tiling],
             recv_sem=peer_recv_sem.at[tiling],
-            device_id=(src, z * 2 + (core + 1) % 2),
+            device_id=(src, z * 2 + core ^ 1),
             device_id_type=MESH,
         )
 
     def forward_copy(tiling, axis):
         half = first_half(axis)
         here = pl.ds(half * QUARTER, QUARTER)
-        to_core = core if axis == 1 else (core + bits(tiling)[1]) % 2
+        to_core = core if axis == 1 else core ^ bits(tiling)[1]
         return pltpu.make_async_remote_copy(
             src_ref=blocks.at[tiling, 2 + axis, here],
             dst_ref=blocks.at[tiling, 5, here],
@@ -409,12 +411,12 @@
 
     def own_slot(tiling, axis):
         v1, v2, v3 = bits(tiling)
-        return (core + (0, v2, v2 + v3)[axis]) % 2
+        return core ^ (0, v2, v2 ^ v3)[axis]
 
     def own_scores(tiling, carry):
         mine = (core, 0, HALF, number(tiling, core))
         score(tiling, mine, mine, True)
-        peer = blocks.at[tiling, (core + 1) % 2]
+        peer = blocks.at[tiling, core ^ 1]
         pltpu.make_async_copy(peer, peer, peer_recv_sem.at[tiling]).wait()
         start = pl.multiple_of(core * QUARTER, QUARTER)
         key = (0, start, QUARTER, number(tiling, 0))
@@ -467,6 +469,44 @@
 
     lax.fori_loop(0, 2, second_scores, 0)
 
+    def stage(kind, slot, tiling):
+        for n in range(HALF // LANES):
+            line = tops[tiling, slot, :, n * LANES : (n + 1) * LANES]
+            shares[tiling * 6 + kind, n : n + 1, :] = line
+
+    def send_found(kind, tiling, target, owner, to_all, send_sem, recv_sem):
+        source = shares.at[tiling * 6 + kind]
+        if kind < 4:
+            place = early.at[owner * 8 + tiling * 4 + kind]
+        else:
+            place = late.at[owner * 4 + tiling * 2 + kind - 4]
+
+        def send_one(m, carry):
+            pltpu.make_async_remote_copy(
+                src_ref=source,
+                dst_ref=place,
+                send_sem=send_sem,
+                recv_sem=recv_sem,
+                device_id=(target, grp_at(m, 1)),
+                device_id_type=MESH,
+            ).start()
+            return carry
+
+        lax.fori_loop(0 if to_all else 1, GRP, send_one, 0)
+        if not to_all:
+            place[...] = source[...]
+
+    for tiling in range(2):
+        v2 = bits(tiling)[1]
+        for kind, slot in enumerate((core, core ^ 1, 3, 4)):
+            stage(kind, slot, tiling)
+        send_found(0, tiling, src, grp, False, early_send_sem, early_recv_sem)
+        send_found(1, tiling, src, grp ^ 1, False, early_send_sem, early_recv_sem)
+        target, owner = device_across(tiling, (1,), core)
+        send_found(2, tiling, target, owner, True, early_send_sem, early_recv_sem)
+        target, owner = device_across(tiling, (2,), core ^ v2)
+        send_found(3, tiling, src, owner, False, early_send_sem, early_recv_sem)
+
     def far_scores(tiling, carry):
         for half in range(2):
             here = blocks.at[tiling, 5, pl.ds(half * QUARTER, QUARTER)]
@@ -477,47 +517,34 @@
     lax.fori_loop(0, 2, far_scores, 0)
 
     for tiling in range(2):
-        v1, v2, v3 = bits(tiling)
-        targets = (
-            ((core + 1) % 2, (), (core + 1) % 2),
-            (2, (0,), (core + v1) % 2),
-            (3, (1,), core),
-            (4, (2,), (core + v2) % 2),
-            (5, (1, 2), core),
-        )
-        for n, (slot, axes, to_core) in enumerate(targets):
-            pltpu.make_async_remote_copy(
-                src_ref=tops.at[tiling, slot],
-                dst_ref=others.at[tiling * 5 + n],
-                send_sem=top_send_sem,
-                recv_sem=top_recv_sem,
-                device_id=device_across(tiling, axes, to_core),
-                device_id_type=MESH,
-            ).start()
-    pltpu.make_async_copy(others, others, top_recv_sem).wait()
-    for tiling in range(2):
-        found = tops[tiling, core]
-        for n in range(5):
-            found = jnp.maximum(found, others[tiling * 5 + n])
-        for n in range(HALF // LANES):
-            line = tiling * (HALF // LANES) + n
-            own_best[line : line + 1, :] = found[:, n * LANES : (n + 1) * LANES]
-
-    best[grp] = own_best[...]
-
-    def send_best(m, carry):
-        pltpu.make_async_remote_copy(
-            src_ref=own_best,
-            dst_ref=best.at[grp],
-            send_sem=best_send_sem,
-            recv_sem=best_recv_sem,
-            device_id=(src, grp_at(m, 1)),
-            device_id_type=MESH,
-        ).start()
-        return carry
-
-    lax.fori_loop(1, GRP, send_best, 0)
-    wait_all(best, best_recv_sem, GRP - 1)
+        v1 = bits(tiling)[0]
+        stage(4, 2, tiling)
+        stage(5, 5, tiling)
+        target, owner = device_across(tiling, (0,), core ^ v1)
+        send_found(4, tiling, target, owner, True, late_send_sem, late_recv_sem)
+        target, owner = device_across(tiling, (1, 2), core)
+        send_found(5, tiling, target, owner, True, late_send_sem, late_recv_sem)
+
+    def wait_early(sem):
+        here = early.at[pl.ds(0, EARLY)]
+        pltpu.make_async_copy(here, here, sem).wait()
+
+    wait_early(early_recv_sem)
+    for owner in range(GRP):
+        for tiling in range(2):
+            line = owner * 8 + tiling * 4
+            early[line] = jnp.maximum(
+                jnp.maximum(early[line], early[line + 1]),
+                jnp.maximum(early[line + 2], early[line + 3]),
+            )
+    pltpu.make_async_copy(late, late, late_recv_sem).wait()
+    for owner in range(GRP):
+        added = []
+        for tiling in range(2):
+            line = owner * 4 + tiling * 2
+            last = jnp.maximum(late[line], late[line + 1])
+            added.append(jnp.maximum(early[owner * 8 + tiling * 4], last))
+        best[owner] = jnp.concatenate(added, axis=0)
 
     answer = jnp.zeros((GRP * rows // LANES, SRC * LANES), F32)
     for piece in three_parts(best[...].reshape(GRP * rows // LANES, LANES)):
@@ -549,8 +576,8 @@
 
     wait_all(sent_meta, column_send_sem, SRC - 1)
     wait_all(group_meta, group_send_sem, GRP - 1)
-    pltpu.make_async_copy(others, others, top_send_sem).wait()
-    wait_all(best, best_send_sem, GRP - 1)
+    wait_early(early_send_sem)
+    pltpu.make_async_copy(late, late, late_send_sem).wait()
     wait_all(answers, answer_send_sem, SRC - 1)
     for n in range(CLASSES):
         first = 1 if n == 0 else 0
@@ -591,8 +618,9 @@
             pltpu.VMEM((2, HELD, HALF, width), BF16),
             pltpu.VMEM((2, HELD, 1, HALF), F32),
             pltpu.VMEM((2, HELD, 1, HALF), jnp.int32),
-            pltpu.VMEM((2 * (HELD - 1), 1, HALF), F32),
-            pltpu.VMEM((rows // LANES, LANES), F32),
+            pltpu.VMEM((12, HALF // LANES, LANES), F32),
+            pltpu.VMEM((GRP * 8, HALF // LANES, LANES), F32),
+            pltpu.VMEM((GRP * 4, HALF // LANES, LANES), F32),
             pltpu.VMEM((GRP, rows // LANES, LANES), F32),
             pltpu.VMEM((SRC, 1, LANES), F32),
             pltpu.VMEM((SRC, 1, LANES), F32),

time: 96.5 us -> 92.9 us (0.963)
  Pallas kernels: 92.2 us -> 88.6 us
    pallas_call x1, Pallas kernels: 92.2 us -> 88.6 us  [on_device(): pl.pallas_call(kernel, out_shape=jax.ShapeDtypeStruct((1, rows), F32), in...]
where the time goes in v4:
time: 92.9 us; the launch traced here: 92.7 us
  Pallas kernels  88.6 us (95%)
  local copies, waits for them, and re-layouts  4.03 us (4%)
    pallas_call x1, Pallas kernels, on_device(): pl.pallas_call(kernel, out_shape=jax.ShapeDtypeStruct((1, rows), F32), in...  88.6 us
    unnamed x9, local copies, waits for them, and re-layouts  4.03 us

profile of v4, /device:TPU:1, one launch (start us, length us, event | category | flops | bytes accessed | tf_op | source)
XLA Modules:
  0.0 92.7 jit_solution(3137279721638270205)
XLA Ops:
  0.0 0.0 copy-start
  0.0 1.4 %copy-done = bf16[1024,768]{1,0:T(8,128)(2,1)S(1)} copy-done((bf16[1024,768]{1,0:T(8,128)(2,1)S(1)}, bf16[1024,768]{1,0:T(8,128)(2,1)}, u32[]{:S(2)}) %copy-start) | copy-done | bytes 1572888
  1.4 0.0 copy-start.1
  1.4 0.7 copy-done.1
  2.1 0.0 copy-start.2
  2.1 0.7 copy-done.2
  2.8 0.0 copy-start.3
  2.8 0.7 copy-done.3
  3.4 88.6 %dedup.1 = f32[1,1024]{1,0:T(1,128)S(1)} custom-call(bf16[1024,768]{1,0:T(8,128)(2,1)S(1)} %copy-done, s32[1,1024]{1,0:T(1,128)S(1)} %bitcast.5, s32[1,1024]{1,0:T(1,128)S(1)} %bitcast.6, s32[1,48]{1,0:T(1,128)S(1)} %bitcast.7), custom_call_target="tpu_custom_call" | custom-call | tf_op jit(solution)/shard_map/dedup/pallas_call | solution.py:599
  92.1 0.6 copy.6
Async XLA Ops:
  0.0 1.4 %copy-start = (bf16[1024,768]{1,0:T(8,128)(2,1)S(1)}, bf16[1024,768]{1,0:T(8,128)(2,1)}, u32[]{:S(2)}) copy-start(bf16[1024,768]{1,0:T(8,128)(2,1)} %embeds_hbm.1) | copy-start | bytes 4718596
  1.4 0.7 copy-start.1
  2.1 0.7 copy-start.2
  2.8 0.7 copy-start.3

commit v5 on v4

--- a/solution.py
+++ b/solution.py
@@ -22,7 +22,7 @@
 HALF = 512
 QUARTER = 256
 HELD = 6
-EARLY = 58
+EARLY = 66
 MIX, UNMIX = 53, 29
 
 NN = (((1,), (0,)), ((), ()))
@@ -110,6 +110,19 @@
     def grp_at(m, sign):
         return ((z + sign * (m >> 1)) & 3) * 2 + ((core + m) & 1)
 
+    barrier = pltpu.get_barrier_semaphore()
+
+    def greet_src(n, carry):
+        pl.semaphore_signal(barrier, inc=1, device_id=(src_at(n, 1), grp), device_id_type=MESH)
+        return carry
+
+    def greet_grp(m, carry):
+        pl.semaphore_signal(barrier, inc=1, device_id=(src, grp_at(m, 1)), device_id_type=MESH)
+        return carry
+
+    lax.fori_loop(1, SRC, greet_src, 0)
+    lax.fori_loop(1, GRP, greet_grp, 0)
+
     loads = []
     for n, (source, target) in enumerate(
         ((ids_hbm, ids), (ranks_hbm, ranks), (sizes_hbm, sizes), (embeds_hbm, embeds))
@@ -117,19 +130,6 @@
         copy = pltpu.make_async_copy(source, target, load_sem.at[n])
         copy.start()
         loads.append(copy)
-
-    barrier = pltpu.get_barrier_semaphore()
-
-    def greet_src(n, carry):
-        pl.semaphore_signal(barrier, inc=1, device_id=(src_at(n, 1), grp), device_id_type=MESH)
-        return carry
-
-    def greet_grp(m, carry):
-        pl.semaphore_signal(barrier, inc=1, device_id=(src, grp_at(m, 1)), device_id_type=MESH)
-        return carry
-
-    lax.fori_loop(1, SRC, greet_src, 0)
-    lax.fori_loop(1, GRP, greet_grp, 0)
 
     for copy in loads[:3]:
         copy.wait()
@@ -469,17 +469,19 @@
 
     lax.fori_loop(0, 2, second_scores, 0)
 
-    def stage(kind, slot, tiling):
+    zero_tiling = x & 1
+    one_tiling = 1 - zero_tiling
+
+    def stage(line, slot, tiling):
         for n in range(HALF // LANES):
-            line = tops[tiling, slot, :, n * LANES : (n + 1) * LANES]
-            shares[tiling * 6 + kind, n : n + 1, :] = line
-
-    def send_found(kind, tiling, target, owner, to_all, send_sem, recv_sem):
-        source = shares.at[tiling * 6 + kind]
-        if kind < 4:
-            place = early.at[owner * 8 + tiling * 4 + kind]
+            shares[line, n : n + 1, :] = tops[tiling, slot, :, n * LANES : (n + 1) * LANES]
+
+    def send_found(line, target, owner, to_all, send_sem, recv_sem):
+        source = shares.at[line]
+        if line < 9:
+            place = early.at[owner * 9 + line]
         else:
-            place = late.at[owner * 4 + tiling * 2 + kind - 4]
+            place = late.at[owner * 2 + line - 9]
 
         def send_one(m, carry):
             pltpu.make_async_remote_copy(
@@ -499,13 +501,17 @@
     for tiling in range(2):
         v2 = bits(tiling)[1]
         for kind, slot in enumerate((core, core ^ 1, 3, 4)):
-            stage(kind, slot, tiling)
-        send_found(0, tiling, src, grp, False, early_send_sem, early_recv_sem)
-        send_found(1, tiling, src, grp ^ 1, False, early_send_sem, early_recv_sem)
+            stage(tiling * 4 + kind, slot, tiling)
+        line = tiling * 4
+        send_found(line, src, grp, False, early_send_sem, early_recv_sem)
+        send_found(line + 1, src, grp ^ 1, False, early_send_sem, early_recv_sem)
         target, owner = device_across(tiling, (1,), core)
-        send_found(2, tiling, target, owner, True, early_send_sem, early_recv_sem)
+        send_found(line + 2, target, owner, True, early_send_sem, early_recv_sem)
         target, owner = device_across(tiling, (2,), core ^ v2)
-        send_found(3, tiling, src, owner, False, early_send_sem, early_recv_sem)
+        send_found(line + 3, src, owner, False, early_send_sem, early_recv_sem)
+    stage(8, 2, one_tiling)
+    target, owner = device_across(one_tiling, (0,), core ^ 1)
+    send_found(8, target, owner, True, early_send_sem, early_recv_sem)
 
     def far_scores(tiling, carry):
         for half in range(2):
@@ -516,14 +522,12 @@
 
     lax.fori_loop(0, 2, far_scores, 0)
 
-    for tiling in range(2):
-        v1 = bits(tiling)[0]
-        stage(4, 2, tiling)
-        stage(5, 5, tiling)
-        target, owner = device_across(tiling, (0,), core ^ v1)
-        send_found(4, tiling, target, owner, True, late_send_sem, late_recv_sem)
-        target, owner = device_across(tiling, (1, 2), core)
-        send_found(5, tiling, target, owner, True, late_send_sem, late_recv_sem)
+    stage(9, 2, zero_tiling)
+    target, owner = device_across(zero_tiling, (0,), core)
+    send_found(9, target, owner, True, late_send_sem, late_recv_sem)
+    stage(10, 5, one_tiling)
+    target, owner = device_across(one_tiling, (1, 2), core)
+    send_found(10, target, owner, True, late_send_sem, late_recv_sem)
 
     def wait_early(sem):
         here = early.at[pl.ds(0, EARLY)]
@@ -532,23 +536,25 @@
     wait_early(early_recv_sem)
     for owner in range(GRP):
         for tiling in range(2):
-            line = owner * 8 + tiling * 4
+            line = owner * 9 + tiling * 4
             early[line] = jnp.maximum(
                 jnp.maximum(early[line], early[line + 1]),
                 jnp.maximum(early[line + 2], early[line + 3]),
             )
     pltpu.make_async_copy(late, late, late_recv_sem).wait()
     for owner in range(GRP):
-        added = []
-        for tiling in range(2):
-            line = owner * 4 + tiling * 2
-            last = jnp.maximum(late[line], late[line + 1])
-            added.append(jnp.maximum(early[owner * 8 + tiling * 4], last))
+        line = owner * 9
+        to_zero, to_one = early[line + 8], jnp.maximum(late[owner * 2], late[owner * 2 + 1])
+        added = (
+            jnp.maximum(early[line], jnp.where(zero_tiling == 0, to_zero, to_one)),
+            jnp.maximum(early[line + 4], jnp.where(zero_tiling == 0, to_one, to_zero)),
+        )
         best[owner] = jnp.concatenate(added, axis=0)
 
-    answer = jnp.zeros((GRP * rows // LANES, SRC * LANES), F32)
-    for piece in three_parts(best[...].reshape(GRP * rows // LANES, LANES)):
-        answer += dot(piece, look[...])
+    lines = GRP * rows // LANES
+    parts = jnp.concatenate(three_parts(best[...].reshape(lines, LANES)), axis=0)
+    answer = dot(parts, look[...])
+    answer = answer[:lines] + answer[lines : 2 * lines] + answer[2 * lines :]
     right = iota(answer.shape, 0) == pick_row
     answer = jnp.sum(jnp.where(right, answer, 0.0), axis=0, keepdims=True)
     for n in range(SRC):
@@ -569,9 +575,8 @@
     lax.fori_loop(1, SRC, send_answer, 0)
     wait_all(returned, answer_recv_sem, SRC - 1)
     table = returned[...].reshape(SRC, LANES).T
-    chosen = jnp.zeros((LANES, rows), F32)
-    for piece in three_parts(table):
-        chosen += dot(piece, to_column)
+    parts = jnp.concatenate(three_parts(table), axis=1)
+    chosen = dot(parts, jnp.concatenate([to_column] * 3, axis=0))
     out[...] = jnp.sum(chosen * lane_hot.astype(F32), axis=0, keepdims=True)
 
     wait_all(sent_meta, column_send_sem, SRC - 1)
@@ -618,9 +623,9 @@
             pltpu.VMEM((2, HELD, HALF, width), BF16),
             pltpu.VMEM((2, HELD, 1, HALF), F32),
             pltpu.VMEM((2, HELD, 1, HALF), jnp.int32),
-            pltpu.VMEM((12, HALF // LANES, LANES), F32),
-            pltpu.VMEM((GRP * 8, HALF // LANES, LANES), F32),
-            pltpu.VMEM((GRP * 4, HALF // LANES, LANES), F32),
+            pltpu.VMEM((11, HALF // LANES, LANES), F32),
+            pltpu.VMEM((GRP * 9, HALF // LANES, LANES), F32),
+            pltpu.VMEM((GRP * 2, HALF // LANES, LANES), F32),
             pltpu.VMEM((GRP, rows // LANES, LANES), F32),
             pltpu.VMEM((SRC, 1, LANES), F32),
             pltpu.VMEM((SRC, 1, LANES), F32),

time: 92.9 us -> 91.7 us (0.987)
  Pallas kernels: 88.6 us -> 87.4 us
    pallas_call x1, Pallas kernels: 88.6 us -> 87.4 us  [on_device(): pl.pallas_call(kernel, out_shape=jax.ShapeDtypeStruct((1, rows), F32), in...]
where the time goes in v5:
time: 91.7 us; the launch traced here: 91.5 us
  Pallas kernels  87.4 us (95%)
  local copies, waits for them, and re-layouts  4.03 us (4%)
    pallas_call x1, Pallas kernels, on_device(): pl.pallas_call(kernel, out_shape=jax.ShapeDtypeStruct((1, rows), F32), in...  87.4 us
    unnamed x9, local copies, waits for them, and re-layouts  4.03 us

profile of v5, /device:TPU:1, one launch (start us, length us, event | category | flops | bytes accessed | tf_op | source)
XLA Modules:
  0.0 91.5 jit_solution(16341717571493219377)
XLA Ops:
  0.0 0.0 copy-start
  0.0 1.4 %copy-done = bf16[1024,768]{1,0:T(8,128)(2,1)S(1)} copy-done((bf16[1024,768]{1,0:T(8,128)(2,1)S(1)}, bf16[1024,768]{1,0:T(8,128)(2,1)}, u32[]{:S(2)}) %copy-start) | copy-done | bytes 1572888
  1.4 0.0 copy-start.1
  1.4 0.7 copy-done.1
  2.1 0.0 copy-start.2
  2.1 0.7 copy-done.2
  2.8 0.0 copy-start.3
  2.8 0.7 copy-done.3
  3.4 87.4 %dedup.1 = f32[1,1024]{1,0:T(1,128)S(1)} custom-call(bf16[1024,768]{1,0:T(8,128)(2,1)S(1)} %copy-done, s32[1,1024]{1,0:T(1,128)S(1)} %bitcast.5, s32[1,1024]{1,0:T(1,128)S(1)} %bitcast.6, s32[1,48]{1,0:T(1,128)S(1)} %bitcast.7), custom_call_target="tpu_custom_call" | custom-call | tf_op jit(solution)/shard_map/dedup/pallas_call | solution.py:604
  90.9 0.6 copy.6
Async XLA Ops:
  0.0 1.4 %copy-start = (bf16[1024,768]{1,0:T(8,128)(2,1)S(1)}, bf16[1024,768]{1,0:T(8,128)(2,1)}, u32[]{:S(2)}) copy-start(bf16[1024,768]{1,0:T(8,128)(2,1)} %embeds_hbm.1) | copy-start | bytes 4718596
  1.4 0.7 copy-start.1
  2.1 0.7 copy-start.2
  2.8 0.7 copy-start.3

commit v6 on v5

--- a/solution.py
+++ b/solution.py
@@ -23,7 +23,7 @@
 QUARTER = 256
 HELD = 6
 EARLY = 66
-MIX, UNMIX = 53, 29
+MIX, UNMIX = 91, 83
 
 NN = (((1,), (0,)), ((), ()))
 NT = (((1,), (1,)), ((), ()))

time: 91.7 us -> 91.3 us (level)
  no operation moved by 1% of the time
where the time goes in v6:
time: 91.3 us; the launch traced here: 91.1 us
  Pallas kernels  87 us (95%)
  local copies, waits for them, and re-layouts  4.03 us (4%)
    pallas_call x1, Pallas kernels, on_device(): pl.pallas_call(kernel, out_shape=jax.ShapeDtypeStruct((1, rows), F32), in...  87 us
    unnamed x9, local copies, waits for them, and re-layouts  4.03 us

profile of v6, /device:TPU:1, one launch (start us, length us, event | category | flops | bytes accessed | tf_op | source)
XLA Modules:
  0.0 91.1 jit_solution(7905568282662875645)
XLA Ops:
  0.0 0.0 copy-start
  0.0 1.4 %copy-done = bf16[1024,768]{1,0:T(8,128)(2,1)S(1)} copy-done((bf16[1024,768]{1,0:T(8,128)(2,1)S(1)}, bf16[1024,768]{1,0:T(8,128)(2,1)}, u32[]{:S(2)}) %copy-start) | copy-done | bytes 1572888
  1.4 0.0 copy-start.1
  1.4 0.7 copy-done.1
  2.1 0.0 copy-start.2
  2.1 0.7 copy-done.2
  2.8 0.0 copy-start.3
  2.8 0.7 copy-done.3
  3.4 87.0 %dedup.1 = f32[1,1024]{1,0:T(1,128)S(1)} custom-call(bf16[1024,768]{1,0:T(8,128)(2,1)S(1)} %copy-done, s32[1,1024]{1,0:T(1,128)S(1)} %bitcast.5, s32[1,1024]{1,0:T(1,128)S(1)} %bitcast.6, s32[1,48]{1,0:T(1,128)S(1)} %bitcast.7), custom_call_target="tpu_custom_call" | custom-call | tf_op jit(solution)/shard_map/dedup/pallas_call | solution.py:604
  90.5 0.6 copy.6
Async XLA Ops:
  0.0 1.4 %copy-start = (bf16[1024,768]{1,0:T(8,128)(2,1)S(1)}, bf16[1024,768]{1,0:T(8,128)(2,1)}, u32[]{:S(2)}) copy-start(bf16[1024,768]{1,0:T(8,128)(2,1)} %embeds_hbm.1) | copy-start | bytes 4718596
  1.4 0.7 copy-start.1
  2.1 0.7 copy-start.2
  2.8 0.7 copy-start.3

commit v7 on v6

--- a/solution.py
+++ b/solution.py
@@ -175,6 +175,17 @@
         sent_meta[n] = meta[n : n + 1, :]
     column_meta[0] = sent_meta[0]
 
+    loads[3].wait()
+
+    def normalise(n, carry):
+        here = pl.ds(pl.multiple_of(n * part, part), part)
+        wide = embeds[here, :].astype(F32)
+        total = jnp.sum(wide * wide, axis=1, keepdims=True)
+        unit[here, :] = (wide * lax.rsqrt(total + epsilon)).astype(BF16)
+        return carry
+
+    lax.fori_loop(0, rows // part, normalise, 0)
+
     pl.semaphore_wait(barrier, SRC - 1 + GRP - 1)
 
     def greet_again(m, carry):
@@ -195,17 +206,6 @@
         return carry
 
     lax.fori_loop(1, SRC, send_column_meta, 0)
-
-    loads[3].wait()
-
-    def normalise(n, carry):
-        here = pl.ds(pl.multiple_of(n * part, part), part)
-        wide = embeds[here, :].astype(F32)
-        total = jnp.sum(wide * wide, axis=1, keepdims=True)
-        unit[here, :] = (wide * lax.rsqrt(total + epsilon)).astype(BF16)
-        return carry
-
-    lax.fori_loop(0, rows // part, normalise, 0)
 
     def wait_all(ref, sem, count):
         pltpu.make_async_copy(ref.at[pl.ds(1, count)], ref.at[pl.ds(1, count)], sem).wait()
@@ -520,11 +520,11 @@
             pair(tiling, (2, 0, HALF), (5, half * QUARTER, QUARTER))
         return carry
 
-    lax.fori_loop(0, 2, far_scores, 0)
-
+    far_scores(zero_tiling, 0)
     stage(9, 2, zero_tiling)
     target, owner = device_across(zero_tiling, (0,), core)
     send_found(9, target, owner, True, late_send_sem, late_recv_sem)
+    far_scores(one_tiling, 0)
     stage(10, 5, one_tiling)
     target, owner = device_across(one_tiling, (1, 2), core)
     send_found(10, target, owner, True, late_send_sem, late_recv_sem)

time: 91.3 us -> 92.1 us (level)
  no operation moved by 1% of the time
where the time goes in v7:
time: 92.1 us; the launch traced here: 91.9 us
  Pallas kernels  87.9 us (95%)
  local copies, waits for them, and re-layouts  4.03 us (4%)
    pallas_call x1, Pallas kernels, on_device(): pl.pallas_call(kernel, out_shape=jax.ShapeDtypeStruct((1, rows), F32), in...  87.9 us
    unnamed x9, local copies, waits for them, and re-layouts  4.03 us

profile of v7, /device:TPU:1, one launch (start us, length us, event | category | flops | bytes accessed | tf_op | source)
XLA Modules:
  0.0 91.9 jit_solution(12313297110086684873)
XLA Ops:
  0.0 0.0 copy-start
  0.0 1.4 %copy-done = bf16[1024,768]{1,0:T(8,128)(2,1)S(1)} copy-done((bf16[1024,768]{1,0:T(8,128)(2,1)S(1)}, bf16[1024,768]{1,0:T(8,128)(2,1)}, u32[]{:S(2)}) %copy-start) | copy-done | bytes 1572888
  1.4 0.0 copy-start.1
  1.4 0.7 copy-done.1
  2.1 0.0 copy-start.2
  2.1 0.7 copy-done.2
  2.8 0.0 copy-start.3
  2.8 0.7 copy-done.3
  3.4 87.9 %dedup.1 = f32[1,1024]{1,0:T(1,128)S(1)} custom-call(bf16[1024,768]{1,0:T(8,128)(2,1)S(1)} %copy-done, s32[1,1024]{1,0:T(1,128)S(1)} %bitcast.5, s32[1,1024]{1,0:T(1,128)S(1)} %bitcast.6, s32[1,48]{1,0:T(1,128)S(1)} %bitcast.7), custom_call_target="tpu_custom_call" | custom-call | tf_op jit(solution)/shard_map/dedup/pallas_call | solution.py:604
  91.3 0.6 copy.6
Async XLA Ops:
  0.0 1.4 %copy-start = (bf16[1024,768]{1,0:T(8,128)(2,1)S(1)}, bf16[1024,768]{1,0:T(8,128)(2,1)}, u32[]{:S(2)}) copy-start(bf16[1024,768]{1,0:T(8,128)(2,1)} %embeds_hbm.1) | copy-start | bytes 4718596
  1.4 0.7 copy-start.1
  2.1 0.7 copy-start.2
  2.8 0.7 copy-start.3
